TPU v7x, 32 devices: a whole 2x2x4 slice. The times are simulated.
32 devices in a mesh: blk: 4 (over y, x), dp: 8 (over z, core).
Axes of the slice: x: 2, y: 2, z: 4, core: 2. Of those that a mesh axis runs over, the one named last changes fastest.
Arguments:
- tokens: bfloat16 [16, 1024, 768], P('dp', 'blk'), may hold values from -6 to 6
- boxes: int32 [4, 16, 1024], P(None, 'dp', 'blk'), may hold values from 0 to 1000
- w_query: bfloat16 [768, 768], replicated, may hold values from -0.21875 to 0.21875
- w_key: bfloat16 [768, 768], replicated, may hold values from -0.21875 to 0.21875
- w_value: bfloat16 [768, 768], replicated, may hold values from -0.21875 to 0.21875
- w_output: bfloat16 [768, 768], replicated, may hold values from -2 to 2
- box_weight: bfloat16 [768, 768], replicated, may hold values from -0.3125 to 0.3125
- first_gain: float32 [768], replicated, may hold values from 0.5 to 1.5
- first_shift: float32 [768], replicated, may hold values from -1.8 to 1.8
- w_expand: bfloat16 [768, 3072], replicated, may hold values from -0.21875 to 0.21875
- w_reduce: bfloat16 [3072, 768], replicated, may hold values from -0.109375 to 0.109375
- second_gain: float32 [768], replicated, may hold values from 0.5 to 1.5
- second_shift: float32 [768], replicated, may hold values from -1.8 to 1.8
- cotangent: bfloat16 [16, 1024, 768], P('dp', 'blk'), may hold values from -6 to 6
Outputs:
- layer_out: bfloat16 [16, 1024, 768], P('dp', 'blk')
- input_grad: bfloat16 [16, 1024, 768], P('dp', 'blk')
- query_grad: float32 [768, 768], replicated
- key_grad: float32 [768, 768], replicated
- value_grad: float32 [768, 768], replicated
- project_grad: float32 [768, 768], replicated
- box_grad: float32 [768, 768], replicated
- first_gain_grad: float32 [768], replicated
- first_shift_grad: float32 [768], replicated
- expand_grad: float32 [768, 3072], replicated
- reduce_grad: float32 [3072, 768], replicated
- second_gain_grad: float32 [768], replicated
- second_shift_grad: float32 [768], replicated
All inputs are finite; a program needn't handle non-finite values.
Results may differ from a plain program's by a relative error of at most 0.018.
Values may be sent and summed in bfloat16 or wider, within the bound.
No kernel may reach another device: no remote copies, remote signals or barrier semaphores. Data moves between devices by JAX's collectives and lax.ppermute only.
A program may use at most 256 MiB of HBM per device.

v0:
```python
import functools

import jax
import jax.numpy as jnp
import numpy as np
from jax import lax
from jax.experimental import pallas as pl
from jax.experimental.pallas import tpu as pltpu
from jax.sharding import PartitionSpec as P

HEADS = 12
HEAD_DIM = 64
HALF = 32
FREQS = 192
CODES = 4 * FREQS
VMEM_LIMIT = 60 * 1024 * 1024
NO_COST = pl.CostEstimate(flops=0, bytes_accessed=0, transcendentals=0)
F32 = jnp.float32
BF16 = jnp.bfloat16


def dot(left, right):
    return lax.dot_general(left, right, (((1,), (0,)), ((), ())), preferred_element_type=F32)


def dot_nt(left, right):
    return lax.dot_general(left, right, (((1,), (1,)), ((), ())), preferred_element_type=F32)


def dot_tn(left, right):
    return lax.dot_general(left, right, (((0,), (0,)), ((), ())), preferred_element_type=F32)


def swapped(block, distance, axis="blk"):
    count = lax.axis_size(axis)
    return lax.ppermute(block, axis, [(i, i ^ distance) for i in range(count)])


def from_blk(block, distance):
    return swapped(block, distance) if distance else block


def from_core(block):
    return swapped(block, 1, "core")


def after(done, value):
    return lax.optimization_barrier((value, done))[0]


def turned(upper, lower, cosines, sines):
    return upper * cosines - lower * sines, lower * cosines + upper * sines


def entry_order(rows):
    return jnp.concatenate(
        [
            rows[:FREQS],
            rows[2 * FREQS : 3 * FREQS],
            rows[FREQS : 2 * FREQS],
            rows[3 * FREQS :],
        ],
        axis=0,
    )


def angle_tables():
    rates = np.float32(10000.0) ** (-np.arange(FREQS, dtype=np.float32) / np.float32(FREQS))
    tables = []
    for places in (32.0 * np.arange(32), 0.5 * np.arange(64)):
        angles = rates.astype(np.float64)[:, None] * places[None, :]
        left = np.concatenate([np.sin(angles), np.cos(angles)])
        parts = []
        for _ in range(3):
            parts.append(left.astype(jnp.bfloat16))
            left = left - parts[-1].astype(np.float64)
        tables.append(np.concatenate(parts, axis=1))
    return tables


def rotary_tables(length):
    rates = np.float32(10000.0) ** (-np.arange(HALF, dtype=np.float32) / np.float32(HALF))
    angles = np.arange(length, dtype=np.float32)[None, :] * rates[:, None]
    angles = angles.astype(np.float64)
    return np.cos(angles).astype(np.float32), np.sin(angles).astype(np.float32)


def prepare_kernel(
    words_ref,
    query_ref,
    key_ref,
    value_ref,
    box_ref,
    cos_ref,
    sin_ref,
    own_ref,
    own_box_ref,
    own_cos_ref,
    own_sin_ref,
):
    rank = words_ref[0]
    span = own_box_ref.shape[0]
    width = query_ref.shape[1]
    count = lax.axis_size("blk")
    block = cos_ref.shape[1] // count
    row = lax.broadcasted_iota(jnp.int32, (span, width), 0) + rank * span
    column = lax.broadcasted_iota(jnp.int32, (span, width), 1)
    pick = jnp.where(row == column, 1.0, 0.0).astype(BF16)
    for kind, ref in enumerate((query_ref, key_ref, value_ref)):
        own_ref[kind * span : (kind + 1) * span] = dot_nt(pick, ref[...]).astype(BF16)
    own_box_ref[...] = dot_nt(pick, entry_order(box_ref[...])).astype(BF16)
    for i in range(count):
        from_cols = pl.ds(pl.multiple_of((rank ^ i) * block, block), block)
        own_cos_ref[:, i * block : (i + 1) * block] = cos_ref[:, from_cols]
        own_sin_ref[:, i * block : (i + 1) * block] = sin_ref[:, from_cols]


def prepare(words, w_query, w_key, w_value, box_weight, span, length):
    width = w_query.shape[0]
    vmem = pl.BlockSpec(memory_space=pltpu.VMEM)
    return pl.pallas_call(
        prepare_kernel,
        in_specs=[pl.BlockSpec(memory_space=pltpu.SMEM)] + [vmem] * 6,
        out_specs=[vmem] * 4,
        out_shape=[
            jax.ShapeDtypeStruct((3 * span, width), BF16),
            jax.ShapeDtypeStruct((span, CODES), BF16),
            jax.ShapeDtypeStruct((HALF, length), F32),
            jax.ShapeDtypeStruct((HALF, length), F32),
        ],
        compiler_params=pltpu.CompilerParams(vmem_limit_bytes=VMEM_LIMIT),
        cost_estimate=pl.CostEstimate(
            flops=8 * span * width * width, bytes_accessed=10 * width * width, transcendentals=0
        ),
        name="prepare",
    )(words, w_query, w_key, w_value, box_weight, *map(jnp.asarray, rotary_tables(length)))


def fold(value, combine):
    while value.shape[0] > 8:
        half = value.shape[0] // 2
        value = combine(value[:half], value[half:])
    return value


def write_codes(page, place_refs, high_ref, low_ref, sin_ref, cos_ref, codes_ref):
    block = sin_ref.shape[1] // len(place_refs)

    def looked_up(table_ref, index):
        spots = table_ref.shape[1] // 3
        rows = lax.broadcasted_iota(jnp.int32, (spots, block), 0).astype(F32)
        once = jnp.where(rows == index, 1.0, 0.0)
        found = dot(table_ref[...], jnp.concatenate([once] * 3, axis=0).astype(BF16))
        return found[:FREQS], found[FREQS:]

    for i, place_ref in enumerate(place_refs):
        columns = slice(i * block, (i + 1) * block)
        places = place_ref[:, :block].astype(F32)
        for axis in range(2):
            at = 4 * page + 2 * axis
            high_sin, high_cos = looked_up(high_ref, places[at : at + 1])
            low_sin, low_cos = looked_up(low_ref, places[at + 1 : at + 2])
            sines = high_sin * low_cos + high_cos * low_sin
            cosines = high_cos * low_cos - high_sin * low_sin
            rows = slice(axis * FREQS, (axis + 1) * FREQS)
            later = slice((2 + axis) * FREQS, (3 + axis) * FREQS)
            sin_ref[rows, columns] = sines
            cos_ref[rows, columns] = cosines
            codes_ref[rows, columns] = sines.astype(BF16)
            codes_ref[later, columns] = cosines.astype(BF16)


def forward_kernel(page, count, words_ref, *refs):
    place_refs, refs = refs[:count], refs[count:]
    piece_refs, refs = refs[:count], refs[count:]
    high_ref, low_ref, w_ref, box_ref, rot_cos_ref, rot_sin_ref = refs[:6]
    probs_ref, att_ref, heads_ref, sin_ref, cos_ref, codes_ref = refs[6:12]
    low_refs = refs[12 : 12 + count]
    tok_ref, pre_ref, kc_ref, qr_ref = refs[12 + count :]
    rows = tok_ref.shape[0]
    block = rows // count
    head = pl.program_id(0)
    span = pl.num_programs(0) * HEAD_DIM

    @pl.when(head == 0)
    def _():
        for i in range(count):
            tok_ref[i * block : (i + 1) * block] = piece_refs[i][...]
        pre_ref[...] = dot_nt(w_ref[...], tok_ref[...])
        write_codes(page, place_refs, high_ref, low_ref, sin_ref, cos_ref, codes_ref)
        kc_ref[:, :CODES] = codes_ref[...].astype(F32).T.astype(BF16)

    def pre(kind):
        at = kind * span + head * HEAD_DIM
        return pre_ref[pl.ds(pl.multiple_of(at, HEAD_DIM), HEAD_DIM)]

    rot_cos = rot_cos_ref[...]
    rot_sin = rot_sin_ref[...]
    query_pre = pre(0).astype(BF16)
    wide = query_pre.astype(F32)
    query = jnp.concatenate(turned(wide[:HALF], wide[HALF:], rot_cos, rot_sin), axis=0)
    key_pre = pre(1)
    key = jnp.concatenate(turned(key_pre[:HALF], key_pre[HALF:], rot_cos, rot_sin), axis=0)
    value = pre(2).astype(BF16)
    heads_ref[0, :HEAD_DIM] = query_pre
    heads_ref[0, HEAD_DIM : 2 * HEAD_DIM] = query.astype(BF16)
    heads_ref[0, 2 * HEAD_DIM : 3 * HEAD_DIM] = key.astype(BF16)
    heads_ref[0, 3 * HEAD_DIM :] = value
    kc_ref[:, CODES:] = key.T.astype(BF16)
    qr_ref[CODES:] = (query * 0.125).astype(BF16)
    step = min(256, block)

    def logits_at(at):
        part = slice(at, at + step)
        projected = dot_tn(box_ref[...], query_pre[:, part])
        sines = sin_ref[:, part]
        cosines = cos_ref[:, part]
        upper = projected[: 2 * FREQS]
        lower = projected[2 * FREQS :]
        qr_ref[: 2 * FREQS, part] = ((upper * cosines + lower * sines) * 0.125).astype(BF16)
        qr_ref[2 * FREQS : CODES, part] = ((lower * cosines - upper * sines) * 0.125).astype(BF16)
        return dot(kc_ref[...], qr_ref[:, part])

    following = logits_at(0)
    for at in range(0, rows, step):
        logits = following
        if at + step < rows:
            following = logits_at(at + step)
        peak = jnp.max(fold(logits, jnp.maximum), axis=0, keepdims=True)
        weight = jnp.exp(logits - peak)
        total = jnp.sum(fold(weight, jnp.add), axis=0, keepdims=True)
        probs = (weight * (1.0 / total)).astype(BF16)
        probs_ref[0, :, at : at + step] = probs
        attended = dot(value, probs)
        att_ref[0, :, at : at + step] = attended
        inner = at % block
        low_refs[at // block][:, inner : inner + step] = attended.astype(BF16)


def fixed(array):
    return pl.BlockSpec(array.shape, lambda *at: (0,) * len(array.shape))


def attention_forward(words, page, messages, pieces, w_own, box_own, rot_cos, rot_sin):
    count = len(messages)
    block, width = messages[0].shape[0] - 16, messages[0].shape[1]
    rows = count * block
    span = box_own.shape[0]
    heads = span // HEAD_DIM
    tables = [jnp.asarray(item) for item in angle_tables()]
    specs = [pl.BlockSpec((block, width), lambda h, words: (0, 0))] * count
    places = pl.BlockSpec((16, width), lambda h, words: (block // 16, 0))
    out_shape = [
        jax.ShapeDtypeStruct((heads, rows, rows), BF16),
        jax.ShapeDtypeStruct((heads, HEAD_DIM, rows), F32),
        jax.ShapeDtypeStruct((heads, 4 * HEAD_DIM, rows), BF16),
        jax.ShapeDtypeStruct((2 * FREQS, rows), F32),
        jax.ShapeDtypeStruct((2 * FREQS, rows), F32),
        jax.ShapeDtypeStruct((CODES, rows), BF16),
    ] + [jax.ShapeDtypeStruct((span, block), BF16)] * count
    return pl.pallas_call(
        functools.partial(forward_kernel, page, count),
        grid_spec=pltpu.PrefetchScalarGridSpec(
            num_scalar_prefetch=1,
            grid=(heads,),
            in_specs=[places] * count
            + specs
            + [fixed(item) for item in (*tables, w_own)]
            + [
                pl.BlockSpec((HEAD_DIM, CODES), lambda h, words: (h, 0)),
                fixed(rot_cos),
                fixed(rot_sin),
            ],
            out_specs=[
                pl.BlockSpec((1, rows, rows), lambda h, words: (h, 0, 0)),
                pl.BlockSpec((1, HEAD_DIM, rows), lambda h, words: (h, 0, 0)),
                pl.BlockSpec((1, 4 * HEAD_DIM, rows), lambda h, words: (h, 0, 0)),
            ]
            + [fixed(item) for item in out_shape[3:6]]
            + [pl.BlockSpec((HEAD_DIM, block), lambda h, words: (h, 0))] * count,
            scratch_shapes=[
                pltpu.VMEM((rows, width), BF16),
                pltpu.VMEM((3 * span, rows), F32),
                pltpu.VMEM((rows, CODES + HEAD_DIM), BF16),
                pltpu.VMEM((CODES + HEAD_DIM, rows), BF16),
            ],
        ),
        out_shape=out_shape,
        compiler_params=pltpu.CompilerParams(vmem_limit_bytes=VMEM_LIMIT),
        cost_estimate=pl.CostEstimate(
            flops=2 * heads * rows * (rows * 1100 + 200 * width + 64 * CODES),
            bytes_accessed=2 * heads * rows * rows + 12 * rows * width,
            transcendentals=heads * rows * rows,
        ),
        name="attention_forward",
    )(words, *messages, *pieces, *tables, w_own, box_own, rot_cos, rot_sin)


def backward_kernel(count, last, words_ref, *refs):
    grad_refs, refs = refs[:count], refs[count:]
    piece_refs, refs = refs[:count], refs[count:]
    probs_ref, att_ref, heads_ref, box_ref, codes_ref, sin_ref, cos_ref = refs[:7]
    rot_cos_ref, rot_sin_ref = refs[7:9]
    refs = refs[9:]
    if last:
        before_ref, refs = refs[0], refs[1:]
    pre_refs, refs = refs[:count], refs[count:]
    if last:
        mine_ref, theirs_ref, *refs = refs
    weight_grad_ref, kc_ref, logit_grad_ref, entry_grad_ref, turned_ref = refs
    block, width = piece_refs[0].shape
    rows = count * block
    head = pl.program_id(0)
    span = pl.num_programs(0) * HEAD_DIM

    @pl.when(head == 0)
    def _():
        kc_ref[:CODES] = codes_ref[...]

    kc_ref[CODES:] = heads_ref[0, 2 * HEAD_DIM : 3 * HEAD_DIM]
    packed = heads_ref[0].astype(F32).T.astype(BF16)
    query_pre = packed[:, :HEAD_DIM]
    query = packed[:, HEAD_DIM : 2 * HEAD_DIM]
    value = packed[:, 3 * HEAD_DIM :] * jnp.asarray(0.125, BF16)
    rot_cos = rot_cos_ref[...]
    rot_sin = rot_sin_ref[...]
    grad = jnp.concatenate([ref[...] for ref in grad_refs], axis=1)
    grad_tall = grad.astype(F32).T.astype(BF16)
    offsets = jnp.sum(grad.astype(F32) * att_ref[0], axis=0, keepdims=True) * 0.125
    step = min(256, block)
    place = pl.multiple_of(head * HEAD_DIM, HEAD_DIM)
    here = pl.ds(place, HEAD_DIM)

    def logits_back(at):
        part = slice(at, at + step)
        grad_probs = dot(value, grad[:, part])
        logit_grad_ref[:, part] = (
            probs_ref[0, :, part].astype(F32) * (grad_probs - offsets[:, part])
        ).astype(BF16)

    logits_back(0)
    for at in range(0, rows, step):
        if at + step < rows:
            logits_back(at + step)
        part = slice(at, at + step)
        back = dot(kc_ref[...], logit_grad_ref[:, part])
        sines = sin_ref[:, part]
        cosines = cos_ref[:, part]
        upper = back[: 2 * FREQS]
        lower = back[2 * FREQS : CODES]
        entry_grad_ref[: 2 * FREQS, part] = (upper * cosines - lower * sines).astype(BF16)
        entry_grad_ref[2 * FREQS :, part] = (lower * cosines + upper * sines).astype(BF16)
        first = back[CODES : CODES + HALF]
        second = back[CODES + HALF :]
        turned_ref[:HALF, part], turned_ref[HALF:, part] = turned(
            first, second, rot_cos[:, part], -rot_sin[:, part]
        )
    key_flat = dot(logit_grad_ref[...], query).T
    value_low = dot(probs_ref[0], grad_tall).T.astype(BF16)
    query_low = (turned_ref[...] + dot(box_ref[...], entry_grad_ref[...])).astype(BF16)
    key_low = jnp.concatenate(
        turned(key_flat[:HALF], key_flat[HALF:], rot_cos, -rot_sin), axis=0
    ).astype(BF16)
    for i in range(count):
        columns = slice(i * block, (i + 1) * block)
        pre_refs[i][here, :block] = query_low[:, columns]
        pre_refs[i][here, block : 2 * block] = key_low[:, columns]
        pre_refs[i][here, 2 * block :] = value_low[:, columns]
    weight_grad_ref[pl.ds(3 * span + place, HEAD_DIM)] = dot(entry_grad_ref[...], query_pre).T

    @pl.when(head == pl.num_programs(0) - 1)
    def _():
        for kind in range(3):
            columns = slice(kind * block, (kind + 1) * block)
            total = dot(pre_refs[0][:, columns], piece_refs[0][...])
            for i in range(1, count):
                total = total + dot(pre_refs[i][:, columns], piece_refs[i][...])
            weight_grad_ref[kind * span : (kind + 1) * span] = total
        if last:
            half = 2 * span
            core = words_ref[2]
            ours = pl.ds(pl.multiple_of(core * half, half), half)
            there = pl.ds(pl.multiple_of((1 - core) * half, half), half)
            mine_ref[...] = weight_grad_ref[ours] + before_ref[ours]
            theirs_ref[...] = (weight_grad_ref[there] + before_ref[there]).astype(BF16)


def attention_backward(
    words, page, grads, pieces, saved, box_own, rot_cos, rot_sin, before=None
):
    probs, att, heads_saved, sines, cosines, codes = saved
    count = len(pieces)
    rows, width = probs.shape[1], pieces[0].shape[1]
    block = rows // count
    span = box_own.shape[0]
    heads = span // HEAD_DIM
    last = before is not None
    extra = (before,) if last else ()
    full_shape = (4 * span, width)
    specs = [pl.BlockSpec((block, width), lambda h, words: (0, 0))] * count
    out_shape = [jax.ShapeDtypeStruct((span, 3 * block), BF16)] * count
    if last:
        out_shape += [
            jax.ShapeDtypeStruct((2 * span, width), F32),
            jax.ShapeDtypeStruct((2 * span, width), BF16),
        ]
    else:
        out_shape.append(jax.ShapeDtypeStruct(full_shape, F32))
    return pl.pallas_call(
        functools.partial(backward_kernel, count, last),
        grid_spec=pltpu.PrefetchScalarGridSpec(
            num_scalar_prefetch=1,
            grid=(heads,),
            in_specs=[pl.BlockSpec((HEAD_DIM, block), lambda h, words: (h, page))] * count
            + specs
            + [
                pl.BlockSpec((1, rows, rows), lambda h, words: (h, 0, 0)),
                pl.BlockSpec((1, HEAD_DIM, rows), lambda h, words: (h, 0, 0)),
                pl.BlockSpec((1, 4 * HEAD_DIM, rows), lambda h, words: (h, 0, 0)),
                pl.BlockSpec((HEAD_DIM, CODES), lambda h, words: (h, 0)),
            ]
            + [fixed(item) for item in (codes, sines, cosines, rot_cos, rot_sin, *extra)],
            out_specs=[fixed(item) for item in out_shape],
            scratch_shapes=([pltpu.VMEM(full_shape, F32)] if last else [])
            + [
                pltpu.VMEM((CODES + HEAD_DIM, rows), BF16),
                pltpu.VMEM((rows, rows), BF16),
                pltpu.VMEM((CODES, rows), BF16),
                pltpu.VMEM((HEAD_DIM, rows), F32),
            ],
        ),
        out_shape=out_shape,
        compiler_params=pltpu.CompilerParams(vmem_limit_bytes=VMEM_LIMIT),
        cost_estimate=pl.CostEstimate(
            flops=2 * heads * rows * (rows * 1400 + 200 * width + 128 * CODES),
            bytes_accessed=2 * heads * rows * rows + 12 * rows * width,
            transcendentals=0,
        ),
        name="attention_backward",
    )(
        words,
        *grads,
        *pieces,
        probs,
        att,
        heads_saved,
        box_own,
        codes,
        sines,
        cosines,
        rot_cos,
        rot_sin,
        *extra,
    )


def normed(value):
    centered = value - jnp.mean(value, axis=-1, keepdims=True)
    scale = lax.rsqrt(jnp.mean(centered * centered, axis=-1, keepdims=True) + 1e-05)
    return centered * scale, scale


def norm_back(grad, gain, unit, scale):
    scaled = grad * gain
    return scale * (
        scaled
        - jnp.mean(scaled, axis=-1, keepdims=True)
        - unit * jnp.mean(scaled * unit, axis=-1, keepdims=True)
    )


def column_sum(value):
    return jnp.sum(value, axis=0, keepdims=True)


def middle_kernel(pages, count, span, chunks, *refs):
    total = pages * count
    words_ref = refs[0]
    att_refs = refs[1 : 1 + total]
    (
        tok_ref,
        cot_ref,
        w_out_ref,
        vectors_ref,
        w_expand_ref,
        w_reduce_ref,
    ) = refs[1 + total : 7 + total]
    outs = refs[7 + total :]
    layer_ref, first_in_ref, theirs_ref, mine_ref, more_theirs_ref, more_mine_ref = outs[:6]
    grad_refs = outs[6 : 6 + count]
    (
        sums_ref,
        att_all,
        grad_all,
        unit_one,
        scale_one,
        first_wide,
        first_low,
        first_tall,
        active,
        slope,
        gathered,
        second_in,
        second_low,
    ) = outs[6 + count :]
    rank = words_ref[0]
    width = tok_ref.shape[1]
    block = tok_ref.shape[0] // pages
    step = pl.program_id(0)

    def rows_of(at):
        return pl.ds(pl.multiple_of((rank ^ at) * span, span), span)

    @pl.when(step == 0)
    def _():
        for page in range(pages):
            for at in range(count):
                att_all[rows_of(at), page * block : (page + 1) * block] = att_refs[
                    page * count + at
                ][...]
        branch = dot_tn(att_all[: w_out_ref.shape[0]], w_out_ref[...])
        unit, scale = normed(tok_ref[...].astype(F32) + branch)
        unit_one[...] = unit
        scale_one[...] = jnp.broadcast_to(scale, scale_one.shape)
        first_out = unit * vectors_ref[0:1] + vectors_ref[1:2]
        first_wide[...] = first_out
        first_low[...] = first_out.astype(BF16)
        first_tall[...] = first_out.T.astype(BF16)
        gathered[...] = jnp.zeros_like(gathered)
        sums_ref[...] = jnp.zeros_like(sums_ref)

    for chunk in range(chunks):

        @pl.when(step == chunk)
        def _(chunk=chunk):
            expanded = dot(first_low[...], w_expand_ref[...])
            gate = 0.5 + 0.5 * lax.erf(expanded * np.float32(np.sqrt(0.5)))
            bell = jnp.exp(expanded * expanded * -0.5) * np.float32(1.0 / np.sqrt(2.0 * np.pi))
            low = (expanded * gate).astype(BF16)
            active[chunk] = low
            slope[chunk] = gate + expanded * bell
            gathered[...] += dot(low, w_reduce_ref[...])

    @pl.when(step == chunks - 1)
    def _():
        unit, scale = normed(first_wide[...] + gathered[...])
        layer_ref[...] = (unit * vectors_ref[2:3] + vectors_ref[3:4]).astype(BF16)
        cot = cot_ref[...].astype(F32)
        sums_ref[2:3] = column_sum(cot * unit)
        sums_ref[3:4] = column_sum(cot)
        grad = norm_back(cot, vectors_ref[2:3], unit, scale)
        second_in[...] = grad
        second_low[...] = grad.astype(BF16)
        gathered[...] = grad

    for chunk in range(chunks):

        @pl.when(step == 2 * chunks - 1 - chunk)
        def _(chunk=chunk):
            grad_active = dot_nt(second_low[...], w_reduce_ref[...])
            grad_expanded = (grad_active * slope[chunk]).astype(BF16)
            grads_ref = mine_ref if chunk < chunks // 2 else theirs_ref
            grads_ref[:width] = dot(first_tall[...], grad_expanded).astype(BF16)
            grads_ref[width:] = dot_tn(active[chunk], second_low[...]).astype(BF16)
            gathered[...] += dot_nt(grad_expanded, w_expand_ref[...])

    @pl.when(step == 2 * chunks - 1)
    def _():
        unit = unit_one[...]
        grad_out = gathered[...]
        sums_ref[0:1] = column_sum(grad_out * unit)
        sums_ref[1:2] = column_sum(grad_out)
        grad = norm_back(grad_out, vectors_ref[0:1], unit, scale_one[:, :1])
        first_in_ref[...] = grad
        low = grad.astype(BF16)
        real = w_out_ref.shape[0]
        half = real // 2
        core = words_ref[2]
        for ref, side in ((more_mine_ref, core), (more_theirs_ref, 1 - core)):
            rows = pl.ds(pl.multiple_of(side * half, half), half)
            ref[:half] = dot(att_all[rows], low).astype(BF16)
            ref[half:] = jnp.zeros((ref.shape[0] - half, width), BF16)
            ref[half : half + 16] = sums_ref[...].astype(BF16)
        if grad_all.shape[0] > real:
            grad_all[real:] = jnp.zeros((grad_all.shape[0] - real, low.shape[0]), BF16)
        grad_all[:real] = dot_nt(w_out_ref[...], low).astype(BF16)
        for at in range(count):
            grad_refs[at][...] = grad_all[rows_of(at)]


def middle(words, att_parts, tok, cot, w_out, vectors, w_expand, w_reduce, pages, more):
    rows, width = tok.shape
    count = len(att_parts) // pages
    span, block = att_parts[0].shape
    hidden = w_expand.shape[1]
    chunks = hidden // width
    pairs = chunks // 2

    def whole(array):
        return pl.BlockSpec(array.shape, lambda s, words: (0,) * len(array.shape))

    def chunk_at(s, words):
        at = jnp.minimum(s, 2 * chunks - 1 - s)
        return (at + words[2] * pairs) % chunks

    def theirs_at(s, words):
        return jnp.clip(2 * chunks - 1 - s - pairs, 0, pairs - 1), 0

    def mine_at(s, words):
        return jnp.clip(2 * chunks - 1 - s, 0, pairs - 1), 0

    shapes = [
        jax.ShapeDtypeStruct((rows, width), BF16),
        jax.ShapeDtypeStruct((rows, width), F32),
        jax.ShapeDtypeStruct((hidden, width), BF16),
        jax.ShapeDtypeStruct((hidden, width), BF16),
        jax.ShapeDtypeStruct((more, width), BF16),
        jax.ShapeDtypeStruct((more, width), BF16),
    ] + [jax.ShapeDtypeStruct((span, pages * block), BF16)] * count
    specs = [whole(item) for item in shapes]
    specs[2] = pl.BlockSpec((2 * width, width), theirs_at)
    specs[3] = pl.BlockSpec((2 * width, width), mine_at)
    return pl.pallas_call(
        functools.partial(middle_kernel, pages, count, span, chunks),
        grid_spec=pltpu.PrefetchScalarGridSpec(
            num_scalar_prefetch=1,
            grid=(2 * chunks,),
            in_specs=[whole(item) for item in att_parts]
            + [
                whole(tok),
                whole(cot),
                whole(w_out),
                whole(vectors),
                pl.BlockSpec((width, width), lambda s, words: (0, chunk_at(s, words))),
                pl.BlockSpec((width, width), lambda s, words: (chunk_at(s, words), 0)),
            ],
            out_specs=specs,
            scratch_shapes=[
                pltpu.VMEM((16, width), F32),
                pltpu.VMEM((count * span, rows), BF16),
                pltpu.VMEM((count * span, rows), BF16),
                pltpu.VMEM((rows, width), F32),
                pltpu.VMEM((rows, 128), F32),
                pltpu.VMEM((rows, width), F32),
                pltpu.VMEM((rows, width), BF16),
                pltpu.VMEM((width, rows), BF16),
                pltpu.VMEM((chunks, rows, width), BF16),
                pltpu.VMEM((chunks, rows, width), F32),
                pltpu.VMEM((rows, width), F32),
                pltpu.VMEM((rows, width), F32),
                pltpu.VMEM((rows, width), BF16),
            ],
        ),
        out_shape=shapes,
        compiler_params=pltpu.CompilerParams(vmem_limit_bytes=VMEM_LIMIT),
        cost_estimate=pl.CostEstimate(
            flops=2 * rows * width * (6 * hidden + 3 * width),
            bytes_accessed=8 * width * hidden + 16 * rows * width,
            transcendentals=2 * rows * hidden,
        ),
        name="middle",
    )(words, *att_parts, tok, cot, w_out, vectors, w_expand, w_reduce)


def input_kernel(pages, count, span, base, *refs):
    words_ref = refs[0]
    own_refs = refs[1 : 1 + pages]
    message_refs = refs[1 + pages : pages + count]
    weight_refs = refs[pages + count : 3 + pages + count]
    first_in_ref, out_ref, held = refs[3 + pages + count :]
    rank = words_ref[0]
    width = out_ref.shape[1]
    block = out_ref.shape[0] // pages
    for page in range(pages):
        for at in range(count):
            part = message_refs[at - 1] if at else own_refs[page]
            top = base + page * span if at else 0
            place = pl.multiple_of((rank ^ at) * span, span)
            for kind in range(3):
                held[kind, pl.ds(place, span), page * block : (page + 1) * block] = part[
                    top : top + span, kind * block : (kind + 1) * block
                ]
    total = dot(weight_refs[0][...], held[0, :width])
    for kind in range(1, 3):
        total = total + dot(weight_refs[kind][...], held[kind, :width])
    out_ref[...] = (first_in_ref[...] + total.T).astype(BF16)


def input_gradient(words, own, messages, base, span, weights, first_in):
    pages = len(own)
    count = 1 + len(messages)
    rows, width = first_in.shape
    vmem = pl.BlockSpec(memory_space=pltpu.VMEM)
    return pl.pallas_call(
        functools.partial(input_kernel, pages, count, span, base),
        in_specs=[pl.BlockSpec(memory_space=pltpu.SMEM)] + [vmem] * (pages + count + 3),
        out_specs=vmem,
        out_shape=jax.ShapeDtypeStruct((rows, width), BF16),
        scratch_shapes=[pltpu.VMEM((3, count * span, rows), BF16)],
        compiler_params=pltpu.CompilerParams(vmem_limit_bytes=VMEM_LIMIT),
        cost_estimate=pl.CostEstimate(
            flops=6 * rows * width * count * span,
            bytes_accessed=2 * width * (5 * rows + 3 * count * span),
            transcendentals=0,
        ),
        name="input_gradient",
    )(words, *own, *messages, *weights, first_in)


def local(body, name, words, arrays, shapes, costly=False):
    def kernel(words_ref, *refs):
        body(words_ref, refs[: len(arrays)], refs[len(arrays) :])

    vmem = pl.BlockSpec(memory_space=pltpu.VMEM)
    shapes = [jax.ShapeDtypeStruct(shape, kind) for shape, kind in shapes]
    moved = sum(item.size * item.dtype.itemsize for item in list(arrays) + shapes)
    cost = pl.CostEstimate(flops=0, bytes_accessed=moved, transcendentals=0)
    return pl.pallas_call(
        kernel,
        in_specs=[pl.BlockSpec(memory_space=pltpu.SMEM)] + [vmem] * len(arrays),
        out_specs=[vmem] * len(shapes),
        out_shape=shapes,
        compiler_params=pltpu.CompilerParams(vmem_limit_bytes=VMEM_LIMIT),
        cost_estimate=cost if costly else NO_COST,
        name=name,
    )(words, *arrays)


def shard(index, rows, base=0):
    return pl.ds(pl.multiple_of(base + index * rows, 16), rows)


def total_of(refs, rows=slice(None)):
    if len(refs) == 2 and all(ref.dtype == BF16 for ref in refs):
        return refs[0][rows] + refs[1][rows]
    total = refs[0][rows].astype(F32)
    for ref in refs[1:]:
        total = total + ref[rows].astype(F32)
    return total


def tree_sum(terms):
    while len(terms) > 1:
        terms = [terms[i] + terms[i + 1] for i in range(0, len(terms), 2)]
    return terms[0]


def bit_of(words, level):
    return lax.shift_right_logical(words[1], level) & 1


def pair_sum(words, mine, other):
    return after(words, mine) + other


def halve(words, level, mine, other):
    rows, width = mine.shape
    half = rows // 2

    def body(words, ins, outs):
        bit = bit_of(words, level)
        outs[0][...] = total_of(ins, shard(bit, half)).astype(BF16)
        outs[1][...] = total_of(ins, shard(1 - bit, half)).astype(BF16)

    return local(body, "halve", words, [mine, other], [((half, width), BF16)] * 2)


def join_halves(words, level, mine, other):
    words, mine = lax.optimization_barrier((words, mine))
    low = bit_of(words, level) == 0
    return jnp.concatenate([jnp.where(low, mine, other), jnp.where(low, other, mine)])


def across(block, level):
    return swapped(block, 1 << level, "depth")


class Plan:
    def __init__(self, rows, rows_a, more, span, width):
        self.count = lax.axis_size("blk")
        self.levels = lax.axis_size("depth").bit_length() - 1
        self.rows = rows
        self.rows_a = rows_a
        self.more = more
        self.span = span
        self.width = width
        self.a_ff = rows_a // self.count
        self.a_more = more // self.count
        self.a = self.a_ff + self.a_more
        self.b = (rows - rows_a) >> self.levels

    def shapes(self, *sizes):
        return [((rows, self.width), BF16) for rows in sizes]

    def scatter_one(self, words, halves):
        count, width = self.count, self.width
        a_ff, a_more = self.a_ff, self.a_more
        b_rows = (self.rows - self.rows_a) // count
        steps = count // 2

        def kernel(words_ref, *refs):
            parts = refs[6 : 6 + count]
            keep_ref, send_ref = refs[6 + count :]
            for i in range(count):

                @pl.when(pl.program_id(0) == i)
                def _(i=i):
                    parts[i][:a_ff] = total_of(refs[:2]).astype(BF16)
                    parts[i][a_ff:] = total_of(refs[2:4]).astype(BF16)
                    side = send_ref if i < steps else keep_ref
                    side[...] = total_of(refs[4:6]).astype(BF16)

        def there(rows):
            return pl.BlockSpec((rows, width), lambda i, words: (words[0] ^ i, 0))

        def b_at(i, words):
            bit = bit_of(words, 0)
            side = jnp.where(i < steps, 1 - bit, bit)
            return self.rows_a // b_rows + side * steps + i % steps, 0

        own_b = pl.BlockSpec((b_rows, width), b_at)
        shapes = [jax.ShapeDtypeStruct((self.a, width), BF16)] * count
        shapes += [jax.ShapeDtypeStruct((b_rows * steps, width), BF16)] * 2
        *parts_a, keep, send = pl.pallas_call(
            kernel,
            grid_spec=pltpu.PrefetchScalarGridSpec(
                num_scalar_prefetch=1,
                grid=(count,),
                in_specs=[there(a_ff)] * 2 + [there(a_more)] * 2 + [own_b] * 2,
                out_specs=[fixed(item) for item in shapes[:count]]
                + [
                    pl.BlockSpec((b_rows, width), lambda i, words: (jnp.maximum(i - steps, 0), 0)),
                    pl.BlockSpec((b_rows, width), lambda i, words: (jnp.minimum(i, steps - 1), 0)),
                ],
            ),
            out_shape=shapes,
            compiler_params=pltpu.CompilerParams(vmem_limit_bytes=VMEM_LIMIT),
            cost_estimate=NO_COST,
            name="scatter_one",
        )(words, *halves, *halves[:2])
        return [from_blk(part, i) for i, part in enumerate(parts_a)], keep, across(send, 0)

    def scatter_two(self, words, parts_a, keep_b, other_b, pages):
        count = self.count
        half = self.a // 2

        def body(words, ins, outs):
            bit = bit_of(words, 0)
            outs[0][...] = total_of(ins[:count], shard(bit, half)).astype(BF16)
            outs[1][...] = total_of(ins[:count], shard(1 - bit, half)).astype(BF16)
            part_b = total_of(ins[count : count + 2]).astype(BF16)
            outs[2][...] = part_b
            for i, out in enumerate(outs[3:]):
                out[: self.b] = part_b
                for page in range(len(pages)):
                    piece = ins[count + 2 + page * (count - 1) + i]
                    base = self.b + page * self.span
                    out[base : base + self.span, : piece.shape[1]] = piece[...]

        message = self.b + len(pages) * self.span
        shapes = self.shapes(half, half, self.b, *[message] * (count - 1))
        pieces = [piece for page in pages for piece in page[1:]]
        keep, send, part_b, *messages = local(
            body, "scatter_two", words, [*parts_a, keep_b, other_b, *pieces], shapes
        )
        return (
            keep,
            across(send, 0),
            part_b,
            [from_blk(item, i + 1) for i, item in enumerate(messages)],
        )

    def sum_b(self, words, part_b, messages):
        def body(words, ins, outs):
            terms = [ref[: self.b].astype(F32) for ref in ins]
            outs[0][...] = tree_sum(terms).astype(BF16)

        return local(body, "sum_b", words, [part_b, *messages], self.shapes(self.b))[0]

    def gather_b(self, words, part_b):
        for level in range(self.levels - 1, 0, -1):
            part_b = join_halves(words, level, part_b, across(part_b, level))
        return part_b, across(part_b, 0)


def gather_blk(part, cut, late=None):
    count = lax.axis_size("blk")
    if count != 4:
        return [(i, 0, from_blk(part, i)) for i in range(count)]
    one, two = swapped(part, 1), swapped(part, 2)
    if late is not None:
        one, two = after(late, (one, two))
    first, second = swapped(one[:cut], 2), swapped(two[cut:], 1)
    return [(0, 0, part), (1, 0, one), (2, 0, two), (3, 0, first), (3, cut, second)]


def with_core(pieces):
    return [(distance, base, from_core(item)) for distance, base, item in pieces]


SEGMENT = 256
SLOTS = 4


def widen_own(words, plan, pieces, halves_b, hidden):
    width = plan.width
    chunks = hidden // width
    pairs = chunks // 2
    per_matrix = width // SEGMENT
    arrays = [item for _, _, item in pieces] + list(halves_b)
    segments = []
    extras = []
    for at, (distance, base, item) in enumerate(pieces):
        stop = min(item.shape[0], plan.a_ff - base)
        for top in range(0, stop, SEGMENT):
            segments.append((at, top, min(SEGMENT, stop - top), distance, base + top))
        if base + item.shape[0] == plan.a:
            extras.append((at, distance))
    for at, item in enumerate(halves_b):
        for top in range(0, item.shape[0], SEGMENT):
            segments.append((len(pieces) + at, top, SEGMENT, None, top))

    def kernel(words_ref, *refs):
        ins = refs[: len(arrays)]
        joined_ref, expand_ref, reduce_ref, held, sems = refs[len(arrays) :]
        copies = []
        for index, (at, top, rows, distance, base) in enumerate(segments):
            slot = index % SLOTS
            if index >= SLOTS:
                copies[index - SLOTS].wait()
            part = ins[at][top : top + rows]
            held[slot, :rows] = part.astype(F32)
            if distance is None:
                half = ins[len(pieces)].shape[0]
                bit = bit_of(words_ref, 0)
                place = plan.rows_a + half * (bit if at == len(pieces) else 1 - bit) + base
            else:
                place = (words_ref[0] ^ distance) * plan.a_ff + base
            joined_ref[pl.ds(pl.multiple_of(place, SEGMENT), rows)] = part
            block = lax.div(place, SEGMENT)
            matrix = lax.div(block, per_matrix)
            row = (block - matrix * per_matrix) * SEGMENT
            chunk = (lax.div(matrix, 2) + words_ref[2] * pairs) % chunks
            column = pl.multiple_of(chunk * width, width)
            source = held.at[slot, :rows]
            to_expand = pltpu.make_async_copy(
                source,
                expand_ref.at[pl.ds(pl.multiple_of(row, SEGMENT), rows), pl.ds(column, width)],
                sems.at[slot],
            )
            to_reduce = pltpu.make_async_copy(
                source,
                reduce_ref.at[pl.ds(pl.multiple_of(column + row, SEGMENT), rows)],
                sems.at[slot],
            )
            is_expand = lax.rem(matrix, 2) == 0
            pl.when(is_expand)(to_expand.start)
            pl.when(jnp.logical_not(is_expand))(to_reduce.start)
            copies.append(to_reduce)
        for at, distance in extras:
            rows = shard(words_ref[0] ^ distance, plan.a_more, plan.rows)
            joined_ref[rows] = ins[at][ins[at].shape[0] - plan.a_more :]
        for copy in copies[-SLOTS:]:
            copy.wait()

    assert all(base % SEGMENT == 0 for *_, base in segments)
    vmem = pl.BlockSpec(memory_space=pltpu.VMEM)
    anywhere = pl.BlockSpec(memory_space=pl.ANY)
    return pl.pallas_call(
        kernel,
        in_specs=[pl.BlockSpec(memory_space=pltpu.SMEM)] + [vmem] * len(arrays),
        out_specs=[vmem, anywhere, anywhere],
        out_shape=[
            jax.ShapeDtypeStruct((plan.rows + plan.more, width), BF16),
            jax.ShapeDtypeStruct((width, hidden), F32),
            jax.ShapeDtypeStruct((hidden, width), F32),
        ],
        scratch_shapes=[
            pltpu.VMEM((SLOTS, SEGMENT, width), F32),
            pltpu.SemaphoreType.DMA((SLOTS,)),
        ],
        compiler_params=pltpu.CompilerParams(vmem_limit_bytes=VMEM_LIMIT),
        cost_estimate=pl.CostEstimate(
            flops=0, bytes_accessed=6 * hidden * width, transcendentals=0
        ),
        name="widen_own",
    )(words, *arrays)


def widen_other(words, joined, expand, reduce):
    width, hidden = expand.shape
    chunks = hidden // width
    pairs = chunks // 2

    def kernel(words_ref, half_ref, before_ref, before_too_ref, expand_ref, reduce_ref):
        expand_ref[...] = half_ref[:width].astype(F32)
        reduce_ref[...] = half_ref[width:].astype(F32)

    def place(s, words):
        return (s + (words[2] + 1) * pairs) % chunks

    anywhere = pl.BlockSpec(memory_space=pl.ANY)
    return pl.pallas_call(
        kernel,
        grid_spec=pltpu.PrefetchScalarGridSpec(
            num_scalar_prefetch=1,
            grid=(pairs,),
            in_specs=[
                pl.BlockSpec((2 * width, width), lambda s, words: (s, 0)),
                anywhere,
                anywhere,
            ],
            out_specs=[
                pl.BlockSpec((width, width), lambda s, words: (0, place(s, words))),
                pl.BlockSpec((width, width), lambda s, words: (place(s, words), 0)),
            ],
        ),
        out_shape=[
            jax.ShapeDtypeStruct((width, hidden), F32),
            jax.ShapeDtypeStruct((hidden, width), F32),
        ],
        input_output_aliases={2: 0, 3: 1},
        compiler_params=pltpu.CompilerParams(vmem_limit_bytes=VMEM_LIMIT),
        cost_estimate=pl.CostEstimate(
            flops=0, bytes_accessed=6 * hidden * width, transcendentals=0
        ),
        name="widen_other",
    )(words, joined, expand, reduce)


def finished(words, plan, heads, joined, side, before=()):
    count = plan.count
    span = plan.span
    width = plan.width
    half_rows = width // 2
    arrays = [item for _, _, item in heads]

    def kernel(words_ref, *refs):
        heads_refs, refs = refs[: len(heads)], refs[len(heads) :]
        extra_ref, refs = refs[0], refs[1 + len(before) :]
        outs, refs = refs[:5], refs[5:]
        gathered, wide, project, sems = refs
        rank = words_ref[0]
        half = words_ref[2] ^ side
        for ref, (distance, base, _) in zip(heads_refs, heads):
            rows = ref.shape[0]
            place = pl.multiple_of((rank ^ distance) * span, HEAD_DIM)
            for part in range(2):
                low, high = max(base, part * span), min(base + rows, (part + 1) * span)
                if low < high:
                    gathered[part, pl.ds(place + (low - part * span), high - low)] = ref[
                        low - base : high - base
                    ]
        for part in range(2):
            wide[part] = gathered[part, :width].astype(F32).T
        project[...] = extra_ref[:half_rows].astype(F32)

        @pl.when(half == 1)
        def _():
            wide[1] = entry_order(wide[1])

        def copy(source, target, at):
            return pltpu.make_async_copy(source, target, sems.at[at])

        for part in range(2):
            pl.when(half == 0)(copy(wide.at[part], outs[part], part).start)
            pl.when(half == 1)(copy(wide.at[part], outs[2 + part], part).start)
        rows = pl.ds(pl.multiple_of(half * half_rows, half_rows), half_rows)
        last = copy(project, outs[4].at[rows], 2)
        last.start()
        for part in range(2):
            copy(wide.at[part], outs[part], part).wait()
        last.wait()

    def whole(item):
        return pl.BlockSpec(item.shape, lambda s: (0, 0))

    more = pl.BlockSpec((plan.more, width), lambda s: (plan.rows // plan.more, 0))
    anywhere = pl.BlockSpec(memory_space=pl.ANY)
    first = 2 + len(heads)
    shapes = [jax.ShapeDtypeStruct((width, width), F32)] * 5
    return pl.pallas_call(
        kernel,
        grid=(1,),
        in_specs=[pl.BlockSpec(memory_space=pltpu.SMEM)]
        + [whole(item) for item in arrays]
        + [more]
        + [anywhere] * len(before),
        out_specs=[anywhere] * 5,
        out_shape=shapes,
        scratch_shapes=[
            pltpu.VMEM((2, count * span, width), BF16),
            pltpu.VMEM((2, width, width), F32),
            pltpu.VMEM((half_rows, width), F32),
            pltpu.SemaphoreType.DMA((3,)),
        ],
        input_output_aliases={first + at: at for at in range(len(before))},
        compiler_params=pltpu.CompilerParams(vmem_limit_bytes=VMEM_LIMIT),
        cost_estimate=pl.CostEstimate(
            flops=0, bytes_accessed=16 * width * width, transcendentals=0
        ),
        name="finish",
    )(words, *arrays, joined, *before)


def per_device(
    tokens,
    boxes,
    w_query,
    w_key,
    w_value,
    w_output,
    box_weight,
    first_gain,
    first_shift,
    w_expand,
    w_reduce,
    second_gain,
    second_shift,
    cotangent,
):
    pages, block, width = tokens.shape
    count = lax.axis_size("blk")
    depth = lax.axis_size("depth")
    words = jnp.stack(
        [lax.axis_index("blk"), lax.axis_index("depth"), lax.axis_index("core")]
    ).astype(jnp.int32)
    hidden = w_expand.shape[1]
    span = -(-HEADS // count) * HEAD_DIM
    unit = 16 * count * depth
    more = -(-(width // 2 + 16) // unit) * unit

    own_places = jnp.stack([boxes[0] + boxes[2], boxes[1] + boxes[3]], axis=1)
    own_places = jnp.stack([lax.shift_right_logical(own_places, 6), own_places & 63], axis=2)
    own_places = own_places.reshape(4 * pages, block).astype(BF16)
    own_places = jnp.pad(own_places, ((0, 16 - 4 * pages), (0, width - block)))
    message = jnp.concatenate([tokens[0], own_places])
    messages = [from_blk(message, i) for i in range(count)]
    w_own, box_own, rot_cos, rot_sin = prepare(
        words, w_query, w_key, w_value, box_weight, span, count * block
    )
    messages, rot_cos = lax.optimization_barrier((messages, rot_cos))
    own = after(messages, tokens[1])
    pieces = [messages, [from_blk(own, i) for i in range(count)]]

    saved = []
    att_parts = []
    for page in range(pages):
        results = attention_forward(
            words, page, messages, pieces[page], w_own, box_own, rot_cos, rot_sin
        )
        saved.append(results[:6])
        att_parts += [from_blk(results[6 + i], i) for i in range(count)]

    vectors = jnp.stack([first_gain, first_shift, second_gain, second_shift])
    results = middle(
        words,
        att_parts,
        tokens.reshape(pages * block, width),
        cotangent.reshape(pages * block, width),
        w_output,
        vectors,
        w_expand,
        w_reduce,
        pages,
        more,
    )
    layer_out, first_in, theirs, mine, more_theirs, more_mine = results[:6]
    grads = [from_blk(results[6 + i], i) for i in range(count)]
    plan = Plan(hidden, 2 * hidden // 3, more, span, width)
    parts_a, keep_b, other_b = plan.scatter_one(
        after(grads[:2], words), [mine, from_core(theirs), more_mine, from_core(more_theirs)]
    )

    def backward(page, words, before=None):
        return attention_backward(
            words,
            page,
            grads,
            pieces[page],
            saved[page],
            box_own,
            rot_cos,
            rot_sin,
            before,
        )

    *pre_one, before = backward(0, after(parts_a[0], words))
    done = before
    for level in range(1, plan.levels):
        keep_b, send_b = halve(after(done, words), level, keep_b, other_b)
        other_b = across(send_b, level)
        done = keep_b
    *pre_two, heads_mine, heads_theirs = backward(1, after(done, words), before)
    own = [pre_one[0], pre_two[0]]
    part_a, other_a, part_b, messages_b = plan.scatter_two(
        after(heads_mine, words), parts_a, keep_b, other_b, [pre_one, pre_two]
    )
    heads, other = halve(
        after(part_a, words), 0, heads_mine, from_core(after(part_a, heads_theirs))
    )
    part_a = pair_sum(after(heads, words), part_a, other_a)
    other = across(after(part_a, other), 0)
    heads = pair_sum(after(part_a, words), heads, other)
    done = heads
    for level in range(1, plan.levels):
        part_a = pair_sum(after(done, words), part_a, across(part_a, level))
        done = part_a
    other_a = across(part_a, 0)
    other = across(heads, 1)
    part_b = plan.sum_b(after(part_a, words), part_b, messages_b)
    heads = pair_sum(after(part_b, words), heads, other)
    part_a = join_halves(after(heads, words), 0, part_a, other_a)
    part_b = after(part_a, part_b)
    for level in range(2, plan.levels):
        heads = pair_sum(words, heads, across(heads, level))
    input_grad = input_gradient(
        after(part_a, words),
        own,
        messages_b,
        plan.b,
        span,
        (w_query, w_key, w_value),
        first_in,
    )
    heads = join_halves(after(input_grad, words), 0, heads, across(heads, 0))
    parts_b = plan.gather_b(after(heads, words), part_b)
    pieces_a = gather_blk(part_a, plan.a_ff // 2, parts_b[0])
    heads = after(([item for _, _, item in pieces_a], parts_b), heads)
    joined, *wide = widen_own(after(heads, words), plan, pieces_a, parts_b, hidden)
    at = plan.rows + width // 2
    sums = [joined[at + i].astype(F32) for i in range(4)]
    pieces_heads = gather_blk(heads, span, (joined, sums))
    joined_other = from_core(after(pieces_heads[1][2], joined))
    grads = finished(words, plan, pieces_heads, joined, 0)
    grad_expand, grad_reduce = widen_other(after(grads, words), joined_other, *wide)
    grad_query, grad_key, grad_value, grad_box, grad_project = finished(
        after(grad_expand, words), plan, with_core(pieces_heads), joined_other, 1, grads
    )
    return (
        layer_out.reshape(tokens.shape),
        input_grad.reshape(tokens.shape),
        grad_query,
        grad_key,
        grad_value,
        grad_project,
        grad_box,
        sums[0],
        sums[1],
        grad_expand,
        grad_reduce,
        sums[2],
        sums[3],
    )


def solution(mesh):
    blocks, rest = mesh.devices.shape
    parts = jax.sharding.Mesh(
        mesh.devices.reshape(blocks, rest // 2, 2), ("blk", "depth", "core")
    )
    split = P(("depth", "core"), "blk", None)
    return jax.shard_map(
        per_device,
        mesh=parts,
        in_specs=(split, P(None, ("depth", "core"), "blk")) + (P(),) * 11 + (split,),
        out_specs=(split, split) + (P(),) * 11,
        check_vma=False,
    )
```

profile of v0, /device:TPU:0, one launch (start us, length us, event | category | flops | bytes accessed | tf_op | source)
XLA Modules:
  0.0 351.7 jit_solution(6375611523639792842)
XLA Ops:
  2.7 4.0 %collective-permute-start.2 = (bf16[272,768]{1,0:T(8,128)(2,1)S(1)}, bf16[272,768]{1,0:T(8,128)(2,1)S(1)}, u32[]{:S(2)}, u32[]{:S(2)}) collective-permute-start(bf16[272,768]{1,0:T(8,128)(2,1)S(1)} %fusion.1.refs_0_.refs_4_), channel_id=1, source_target_pairs={{0,24},{8,16},{16,8},{24,0},{1,25},{9,17},{17,9},{25,1},{2,26},{10... | collective-permute-start | bytes 1253384 | tf_op jit(solution)/shard_map/ppermute | solution.py:36
  8.1 4.9 %prepare.1 = (bf16[576,768]{1,0:T(8,128)(2,1)}, bf16[192,768]{1,0:T(8,128)(2,1)}, f32[32,1024]{1,0:T(8,128)}, f32[32,1024]{1,0:T(8,128)}) custom-call(s32[3]{0:T(128)} %pad_add_fusion.1.words_ref.refs_0_, bf16[768,768]{1,0:T(8,128)(2,1)} %refs_6_.1, bf16[768,768]{1,0:T(8,128)(2,1)} %refs_7_.1, bf16[768,768]{1,0:T(8,128)(2,1)} %refs_8_.3, ...), custom_call_target="tpu_custom_call" | custom-call | flops 905969664 | bytes 5898240 | tf_op jit(solution)/shard_map/prepare/pallas_call | solution.py:121
  13.0 4.2 %collective-permute-done.2.refs_3_.refs_7_ = bf16[272,768]{1,0:T(8,128)(2,1)S(1)} collective-permute-done((bf16[272,768]{1,0:T(8,128)(2,1)S(1)}, bf16[272,768]{1,0:T(8,128)(2,1)S(1)}, u32[]{:S(2)}, u32[]{:S(2)}) %collective-permute-start.2) | collective-permute-done | bytes 417824 | tf_op jit(solution)/shard_map/ppermute | solution.py:36
  17.2 8.1 %collective-permute-done.1.refs_2_.refs_6_ = bf16[272,768]{1,0:T(8,128)(2,1)S(1)} collective-permute-done((bf16[272,768]{1,0:T(8,128)(2,1)S(1)}, bf16[272,768]{1,0:T(8,128)(2,1)S(1)}, u32[]{:S(2)}, u32[]{:S(2)}) %collective-permute-start.1) | collective-permute-done | bytes 417824 | tf_op jit(solution)/shard_map/ppermute | solution.py:36
  29.1 21.2 %attention_forward.2 = (bf16[3,1024,1024]{2,1,0:T(8,128)(2,1)}, f32[3,64,1024]{2,1,0:T(8,128)}, bf16[3,256,1024]{2,1,0:T(8,128)(2,1)}, f32[384,1024]{1,0:T(8,128...) custom-call(s32[3]{0:T(128)} %pad_add_fusion.1.words_ref.refs_0_, ...), custom_call_target="tpu_custom_call" | custom-call | flops 8166309888 | bytes 15728640 | tf_op jit(solution)/shard_map/attention_forward/pallas_call | solution.py:261
  55.3 21.2 %attention_forward.3 = (bf16[3,1024,1024]{2,1,0:T(8,128)(2,1)}, f32[3,64,1024]{2,1,0:T(8,128)}, bf16[3,256,1024]{2,1,0:T(8,128)(2,1)}, f32[384,1024]{1,0:T(8,128...) custom-call(s32[3]{0:T(128)} %pad_add_fusion.1.words_ref.refs_0_, ...), custom_call_target="tpu_custom_call" | custom-call | flops 8166309888 | bytes 15728640 | tf_op jit(solution)/shard_map/attention_forward/pallas_call | solution.py:261
  85.1 43.1 %middle.1 = (bf16[512,768]{1,0:T(8,128)(2,1)}, f32[512,768]{1,0:T(8,128)}, bf16[3072,768]{1,0:T(8,128)(2,1)}, bf16[3072,768]{1,0:T(8,128)(2,1)}, bf16[512,768]{1...) custom-call(s32[3]{0:T(128)} %pad_add_fusion.1.words_ref.refs_0_, ...), custom_call_target="tpu_custom_call" | custom-call | flops 16307453952 | bytes 25165824 | tf_op jit(solution)/shard_map/middle/pallas_call | solution.py:623
  132.3 4.5 %collective-permute-done.12.refs_1_ = bf16[192,512]{1,0:T(8,128)(2,1)S(1)} collective-permute-done((bf16[192,512]{1,0:T(8,128)(2,1)}, bf16[192,512]{1,0:T(8,128)(2,1)S(1)}, u32[]{:S(2)}, u32[]{:S(2)}) %collective-permute-start.12) | collective-permute-done | bytes 196640 | tf_op jit(solution)/shard_map/ppermute | solution.py:36
  137.7 7.9 %scatter_one.1 = (bf16[640,768]{1,0:T(8,128)(2,1)}, bf16[640,768]{1,0:T(8,128)(2,1)}, bf16[640,768]{1,0:T(8,128)(2,1)}, bf16[640,768]{1,0:T(8,128)(2,1)}, bf16[5...) custom-call(s32[3]{0:T(128)} %pad_add_fusion.1.words_ref.refs_0_, bf16[3072,768]{1,0:T(8,128)(2,1)} %get-tuple-element.146.refs_0_.refs_4_, ...), custom_call_target="tpu_custom_call" | custom-call | tf_op jit(solution)/shard_map/scatter_one/pallas_call | solution.py:824
  150.8 22.0 %attention_backward.2 = (bf16[192,768]{1,0:T(8,128)(2,1)}, bf16[192,768]{1,0:T(8,128)(2,1)}, bf16[192,768]{1,0:T(8,128)(2,1)}, bf16[192,768]{1,0:T(8,128)(2,1)}, f32[768,768]{1,0:T(8,128)}) custom-call(s32[3]{0:T(128)} %pad_add_fusion.1.words_ref.refs_0_, bf16[192,512]{1,0:T(8,128)(2,1)} %get-tuple-element.143.refs_0_, bf16[192,512]{1,0:T(8,128)(2,1)} %copy-done.37, ...), custom_call_target="tpu_custom_call" | custom-call | flops 10355736576 | bytes 15728640 | tf_op jit(solution)/shard_map/attention_backward/pallas_call | solution.py:409
  178.6 23.0 %attention_backward.3 = (bf16[192,768]{1,0:T(8,128)(2,1)}, bf16[192,768]{1,0:T(8,128)(2,1)}, bf16[192,768]{1,0:T(8,128)(2,1)}, bf16[192,768]{1,0:T(8,128)(2,1)},...) custom-call(s32[3]{0:T(128)} %pad_add_fusion.1.words_ref.refs_0_, bf16[192,512]{1,0:T(8,128)(2,1)} %get-tuple-element.143.refs_0_, ...), custom_call_target="tpu_custom_call" | custom-call | flops 10355736576 | bytes 15728640 | tf_op jit(solution)/shard_map/attention_backward/pallas_call | solution.py:409
  203.4 5.2 %scatter_two.1 = (bf16[320,768]{1,0:T(8,128)(2,1)}, bf16[320,768]{1,0:T(8,128)(2,1)}, bf16[256,768]{1,0:T(8,128)(2,1)}, bf16[640,768]{1,0:T(8,128)(2,1)}, bf16[6...) custom-call(s32[3]{0:T(128)} %pad_add_fusion.1.words_ref.refs_0_, bf16[640,768]{1,0:T(8,128)(2,1)} %get-tuple-element.150.refs_0_, ...), custom_call_target="tpu_custom_call" | custom-call | tf_op jit(solution)/shard_map/scatter_two/pallas_call | solution.py:718
  212.6 8.2 %collective-permute-done.23 = bf16[320,768]{1,0:T(8,128)(2,1)S(1)} collective-permute-done((bf16[320,768]{1,0:T(8,128)(2,1)}, bf16[320,768]{1,0:T(8,128)(2,1)S(1)}, u32[]{:S(2)}, u32[]{:S(2)}) %collective-permute-start.23) | collective-permute-done | bytes 491552 | tf_op jit(solution)/shard_map/ppermute | solution.py:36
  225.0 19.3 %collective-permute-done.26 = bf16[320,768]{1,0:T(8,128)(2,1)} collective-permute-done((bf16[320,768]{1,0:T(8,128)(2,1)S(1)}, bf16[320,768]{1,0:T(8,128)(2,1)}, u32[]{:S(2)}, u32[]{:S(2)}) %collective-permute-start.26) | collective-permute-done | bytes 491552 | tf_op jit(solution)/shard_map/ppermute | solution.py:36
  247.5 7.9 %collective-permute-done.29.refs_4_.refs_2_ = bf16[640,768]{1,0:T(8,128)(2,1)S(1)} collective-permute-done((bf16[640,768]{1,0:T(8,128)(2,1)}, bf16[640,768]{1,0:T(8,128)(2,1)S(1)}, u32[]{:S(2)}, u32[]{:S(2)}) %collective-permute-start.29) | collective-permute-done | bytes 983072 | tf_op jit(solution)/shard_map/ppermute | solution.py:36
  259.6 3.2 collective-permute-done.25
  270.6 6.9 %input_gradient.1 = bf16[512,768]{1,0:T(8,128)(2,1)} custom-call(s32[3]{0:T(128)} %pad_add_fusion.1.words_ref.refs_0_, bf16[192,768]{1,0:T(8,128)(2,1)} %get-tuple-element.196.refs_1_, bf16[192,768]{1,0:T(8,128)(2,1)} %get-tuple-element.197.refs_2_, bf16[640,768]{1,0:T(8,128)(2,1)} %copy-done.1, bf16[640,768]{1,0:T(8,128)(2,1)} %copy-done.2, ...), custom_call_target="tpu_custom_call" | custom-call | flops 1811939328 | bytes 7471104 | tf_op jit(solution)/shard_map/input_gradient/pallas_call | solution.py:694
  280.2 7.4 %collective-permute-done.34 = bf16[256,768]{1,0:T(8,128)(2,1)S(1)} collective-permute-done((bf16[256,768]{1,0:T(8,128)(2,1)S(1)}, bf16[256,768]{1,0:T(8,128)(2,1)S(1)}, u32[]{:S(2)}, u32[]{:S(2)}) %collective-permute-start.34) | collective-permute-done | bytes 393248 | tf_op jit(solution)/shard_map/ppermute | solution.py:36
  293.9 11.8 %collective-permute-done.37.refs_6_ = bf16[512,768]{1,0:T(8,128)(2,1)S(1)} collective-permute-done((bf16[512,768]{1,0:T(8,128)(2,1)S(1)}, bf16[512,768]{1,0:T(8,128)(2,1)S(1)}, u32[]{:S(2)}, u32[]{:S(2)}) %collective-permute-start.37) | collective-permute-done | bytes 786464 | tf_op jit(solution)/shard_map/ppermute | solution.py:36
  309.2 8.7 %widen_own.1 = (bf16[3584,768]{1,0:T(8,128)(2,1)}, f32[768,3072]{1,0:T(8,128)}, f32[3072,768]{1,0:T(8,128)}) custom-call(s32[3]{0:T(128)} %pad_add_fusion.1.words_ref.refs_0_, bf16[640,768]{1,0:T(8,128)(2,1)} %copy-done, bf16[640,768]{1,0:T(8,128)(2,1)} %collective-permute-done.32.refs_1_, bf16[640,768]{1,0:T(8,128)(2,1)} %copy-done.5, ...), custom_call_target="tpu_custom_call" | custom-call | bytes 14155776 | tf_op jit(solution)/shard_map/widen_own/pallas_call | solution.py:969
  324.4 6.7 %collective-permute-done.40.refs_3_ = bf16[192,768]{1,0:T(8,128)(2,1)S(1)} collective-permute-done((bf16[192,768]{1,0:T(8,128)(2,1)S(1)}, bf16[192,768]{1,0:T(8,128)(2,1)S(1)}, u32[]{:S(2)}, u32[]{:S(2)}) %collective-permute-start.40) | collective-permute-done | bytes 294944 | tf_op jit(solution)/shard_map/ppermute | solution.py:36
  332.6 5.3 %finish.2 = (f32[768,768]{1,0:T(8,128)}, f32[768,768]{1,0:T(8,128)}, f32[768,768]{1,0:T(8,128)}, f32[768,768]{1,0:T(8,128)}, f32[768,768]{1,0:T(8,128)}) custom-call(s32[3]{0:T(128)} %pad_add_fusion.1.words_ref.refs_0_, bf16[384,768]{1,0:T(8,128)(2,1)} %copy-done.6, bf16[384,768]{1,0:T(8,128)(2,1)} %copy-done.9, bf16[384,768]{1,0:T(8,128)(2,1)} %copy-done.8, ...), custom_call_target="tpu_custom_call" | custom-call | bytes 9437184 | tf_op jit(solution)/shard_map/finish/pallas_call | solution.py:1082
  337.9 6.2 %widen_other.1 = (f32[768,3072]{1,0:T(8,128)}, f32[3072,768]{1,0:T(8,128)}) custom-call(s32[3]{0:T(128)} %pad_add_fusion.1.words_ref.refs_0_, bf16[3584,768]{1,0:T(8,128)(2,1)} %collective-permute-done.42.half_ref.refs_5_, f32[768,3072]{1,0:T(8,128)} %get-tuple-element.225.before_ref, ...), custom_call_target="tpu_custom_call", output_to_operand_aliasing={{0}: (2, {}), {1}: (3, {})} | custom-call | bytes 14155776 | tf_op jit(solution)/shard_map/widen_other/pallas_call | solution.py:1003
  346.1 5.4 %finish.3 = (f32[768,768]{1,0:T(8,128)}, f32[768,768]{1,0:T(8,128)}, f32[768,768]{1,0:T(8,128)}, f32[768,768]{1,0:T(8,128)}, f32[768,768]{1,0:T(8,128)}) custom-call(s32[3]{0:T(128)} %pad_add_fusion.1.words_ref.refs_0_, bf16[384,768]{1,0:T(8,128)(2,1)} %copy-done.16, ...), custom_call_target="tpu_custom_call", output_to_operand_aliasing={{0}: (7, {}), {1}: (8, {}), {2}: (9, {}), {3}: (10, {}), {4... | custom-call | bytes 9437184 | tf_op jit(solution)/shard_map/finish/pallas_call | solution.py:1082
  (209 shorter events, 82.2 us)
Async XLA Ops:
  25.6 26.9 %collective-permute-start.8 = (bf16[256,768]{1,0:T(8,128)(2,1)S(1)}, bf16[256,768]{1,0:T(8,128)(2,1)S(1)}, u32[]{:S(2)}, u32[]{:S(2)}) collective-permute-start(bf16[256,768]{1,0:T(8,128)(2,1)S(1)} %get-tuple-element.137.refs_4_), channel_id=1, source_target_pairs={{0,24},{8,16},{16,8},{24,0},{1,25},{9,17},{17,9},{25,1},{2,26},{10... | collective-permute-start | bytes 1179656 | tf_op jit(solution)/shard_map/ppermute | solution.py:36
  27.2 26.7 %collective-permute-start.7 = (bf16[256,768]{1,0:T(8,128)(2,1)S(1)}, bf16[256,768]{1,0:T(8,128)(2,1)S(1)}, u32[]{:S(2)}, u32[]{:S(2)}) collective-permute-start(bf16[256,768]{1,0:T(8,128)(2,1)S(1)} %get-tuple-element.137.refs_4_), channel_id=1, source_target_pairs={{0,16},{8,24},{16,0},{24,8},{1,17},{9,25},{17,1},{25,9},{2,18},{10... | collective-permute-start | bytes 1179656 | tf_op jit(solution)/shard_map/ppermute | solution.py:36
  28.5 25.3 %collective-permute-start.6 = (bf16[256,768]{1,0:T(8,128)(2,1)S(1)}, bf16[256,768]{1,0:T(8,128)(2,1)S(1)}, u32[]{:S(2)}, u32[]{:S(2)}) collective-permute-start(bf16[256,768]{1,0:T(8,128)(2,1)S(1)} %get-tuple-element.137.refs_4_), channel_id=1, source_target_pairs={{0,8},{8,0},{16,24},{24,16},{1,9},{9,1},{17,25},{25,17},{2,10},{10... | collective-permute-start | bytes 1179656 | tf_op jit(solution)/shard_map/ppermute | solution.py:36
  50.3 28.5 %collective-permute-start.3 = (bf16[192,256]{1,0:T(8,128)(2,1)}, bf16[192,256]{1,0:T(8,128)(2,1)S(1)}, u32[]{:S(2)}, u32[]{:S(2)}) collective-permute-start(bf16[192,256]{1,0:T(8,128)(2,1)} %get-tuple-element.134), channel_id=1, source_target_pairs={{0,8},{8,0},{16,24},{24,16},{1,9},{9,1},{17,25},{25,17},{2,10},{10... | collective-permute-start | bytes 294920 | tf_op jit(solution)/shard_map/ppermute | solution.py:36
  51.8 28.9 %collective-permute-start.4 = (bf16[192,256]{1,0:T(8,128)(2,1)}, bf16[192,256]{1,0:T(8,128)(2,1)S(1)}, u32[]{:S(2)}, u32[]{:S(2)}) collective-permute-start(bf16[192,256]{1,0:T(8,128)(2,1)} %get-tuple-element.135), channel_id=1, source_target_pairs={{0,16},{8,24},{16,0},{24,8},{1,17},{9,25},{17,1},{25,9},{2,18},{10... | collective-permute-start | bytes 294920 | tf_op jit(solution)/shard_map/ppermute | solution.py:36
  52.5 28.2 %collective-permute-start.5 = (bf16[192,256]{1,0:T(8,128)(2,1)}, bf16[192,256]{1,0:T(8,128)(2,1)S(1)}, u32[]{:S(2)}, u32[]{:S(2)}) collective-permute-start(bf16[192,256]{1,0:T(8,128)(2,1)} %get-tuple-element.136), channel_id=1, source_target_pairs={{0,24},{8,16},{16,8},{24,0},{1,25},{9,17},{17,9},{25,1},{2,26},{10... | collective-permute-start | bytes 294920 | tf_op jit(solution)/shard_map/ppermute | solution.py:36
  130.1 18.9 %collective-permute-start.15 = (bf16[192,512]{1,0:T(8,128)(2,1)}, bf16[192,512]{1,0:T(8,128)(2,1)S(1)}, u32[]{:S(2)}, u32[]{:S(2)}) collective-permute-start(bf16[192,512]{1,0:T(8,128)(2,1)} %get-tuple-element.152), channel_id=1, source_target_pairs={{0,16},{8,24},{16,0},{24,8},{1,17},{9,25},{17,1},{25,9},{2,18},{10... | collective-permute-start | bytes 589832 | tf_op jit(solution)/shard_map/ppermute | solution.py:36
  130.7 20.1 %collective-permute-start.16 = (bf16[192,512]{1,0:T(8,128)(2,1)}, bf16[192,512]{1,0:T(8,128)(2,1)}, u32[]{:S(2)}, u32[]{:S(2)}) collective-permute-start(bf16[192,512]{1,0:T(8,128)(2,1)} %get-tuple-element.153), channel_id=1, source_target_pairs={{0,24},{8,16},{16,8},{24,0},{1,25},{9,17},{17,9},{25,1},{2,26},{10... | collective-permute-start | bytes 589832 | tf_op jit(solution)/shard_map/ppermute | solution.py:36
  145.5 27.3 %collective-permute-start.17 = (bf16[512,768]{1,0:T(8,128)(2,1)}, bf16[512,768]{1,0:T(8,128)(2,1)S(1)}, u32[]{:S(2)}, u32[]{:S(2)}) collective-permute-start(bf16[512,768]{1,0:T(8,128)(2,1)} %get-tuple-element.163), channel_id=1, source_target_pairs={{0,2},{2,0},{4,6},{6,4},{1,3},{3,1},{5,7},{7,5},{8,10},{10,8},{12,... | collective-permute-start | bytes 2359304 | tf_op jit(solution)/shard_map/ppermute | solution.py:36
  147.3 54.3 %collective-permute-start.18 = (bf16[640,768]{1,0:T(8,128)(2,1)}, bf16[640,768]{1,0:T(8,128)(2,1)S(1)}, u32[]{:S(2)}, u32[]{:S(2)}) collective-permute-start(bf16[640,768]{1,0:T(8,128)(2,1)} %get-tuple-element.174), channel_id=1, source_target_pairs={{0,8},{8,0},{16,24},{24,16},{1,9},{9,1},{17,25},{25,17},{2,10},{10... | collective-permute-start | bytes 2949128 | tf_op jit(solution)/shard_map/ppermute | solution.py:36
  148.5 53.1 %collective-permute-start.19 = (bf16[640,768]{1,0:T(8,128)(2,1)}, bf16[640,768]{1,0:T(8,128)(2,1)S(1)}, u32[]{:S(2)}, u32[]{:S(2)}) collective-permute-start(bf16[640,768]{1,0:T(8,128)(2,1)} %get-tuple-element.175), channel_id=1, source_target_pairs={{0,16},{8,24},{16,0},{24,8},{1,17},{9,25},{17,1},{25,9},{2,18},{10... | collective-permute-start | bytes 2949128 | tf_op jit(solution)/shard_map/ppermute | solution.py:36
  149.1 52.6 %collective-permute-start.20 = (bf16[640,768]{1,0:T(8,128)(2,1)}, bf16[640,768]{1,0:T(8,128)(2,1)S(1)}, u32[]{:S(2)}, u32[]{:S(2)}) collective-permute-start(bf16[640,768]{1,0:T(8,128)(2,1)} %get-tuple-element.176), channel_id=1, source_target_pairs={{0,24},{8,16},{16,8},{24,0},{1,25},{9,17},{17,9},{25,1},{2,26},{10... | collective-permute-start | bytes 2949128 | tf_op jit(solution)/shard_map/ppermute | solution.py:36
  176.1 25.6 %collective-permute-start.21 = (bf16[256,768]{1,0:T(8,128)(2,1)}, bf16[256,768]{1,0:T(8,128)(2,1)S(1)}, u32[]{:S(2)}, u32[]{:S(2)}) collective-permute-start(bf16[256,768]{1,0:T(8,128)(2,1)} %get-tuple-element.177), channel_id=1, source_target_pairs={{0,4},{2,6},{4,0},{6,2},{1,5},{3,7},{5,1},{7,3},{8,12},{10,14},{12... | collective-permute-start | bytes 1179656 | tf_op jit(solution)/shard_map/ppermute | solution.py:36
  209.1 38.5 %collective-permute-start.28 = (bf16[640,768]{1,0:T(8,128)(2,1)}, bf16[640,768]{1,0:T(8,128)(2,1)S(1)}, u32[]{:S(2)}, u32[]{:S(2)}) collective-permute-start(bf16[640,768]{1,0:T(8,128)(2,1)} %get-tuple-element.198), channel_id=1, source_target_pairs={{0,8},{8,0},{16,24},{24,16},{1,9},{9,1},{17,25},{25,17},{2,10},{10... | collective-permute-start | bytes 2949128 | tf_op jit(solution)/shard_map/ppermute | solution.py:36
  210.3 45.2 %collective-permute-start.29 = (bf16[640,768]{1,0:T(8,128)(2,1)}, bf16[640,768]{1,0:T(8,128)(2,1)S(1)}, u32[]{:S(2)}, u32[]{:S(2)}) collective-permute-start(bf16[640,768]{1,0:T(8,128)(2,1)} %get-tuple-element.199), channel_id=1, source_target_pairs={{0,16},{8,24},{16,0},{24,8},{1,17},{9,25},{17,1},{25,9},{2,18},{10... | collective-permute-start | bytes 2949128 | tf_op jit(solution)/shard_map/ppermute | solution.py:36
  210.9 44.6 %collective-permute-start.30 = (bf16[640,768]{1,0:T(8,128)(2,1)}, bf16[640,768]{1,0:T(8,128)(2,1)S(1)}, u32[]{:S(2)}, u32[]{:S(2)}) collective-permute-start(bf16[640,768]{1,0:T(8,128)(2,1)} %get-tuple-element.200), channel_id=1, source_target_pairs={{0,24},{8,16},{16,8},{24,0},{1,25},{9,17},{17,9},{25,1},{2,26},{10... | collective-permute-start | bytes 2949128 | tf_op jit(solution)/shard_map/ppermute | solution.py:36
  221.9 22.4 %collective-permute-start.26 = (bf16[320,768]{1,0:T(8,128)(2,1)S(1)}, bf16[320,768]{1,0:T(8,128)(2,1)}, u32[]{:S(2)}, u32[]{:S(2)}) collective-permute-start(bf16[320,768]{1,0:T(8,128)(2,1)S(1)} %add.56), channel_id=1, source_target_pairs={{0,4},{2,6},{4,0},{6,2},{1,5},{3,7},{5,1},{7,3},{8,12},{10,14},{12... | collective-permute-start | bytes 1474568 | tf_op jit(solution)/shard_map/ppermute | solution.py:36
  224.6 20.9 %collective-permute-start.24 = (bf16[192,768]{1,0:T(8,128)(2,1)}, bf16[192,768]{1,0:T(8,128)(2,1)S(1)}, u32[]{:S(2)}, u32[]{:S(2)}) collective-permute-start(bf16[192,768]{1,0:T(8,128)(2,1)} %get-tuple-element.191), channel_id=1, source_target_pairs={{0,2},{2,0},{4,6},{6,4},{1,3},{3,1},{5,7},{7,5},{8,10},{10,8},{12,... | collective-permute-start | bytes 884744 | tf_op jit(solution)/shard_map/ppermute | solution.py:36
  245.5 20.3 %collective-permute-start.27 = (bf16[320,768]{1,0:T(8,128)(2,1)S(1)}, bf16[320,768]{1,0:T(8,128)(2,1)}, u32[]{:S(2)}, u32[]{:S(2)}) collective-permute-start(bf16[320,768]{1,0:T(8,128)(2,1)S(1)} %add.59), channel_id=1, source_target_pairs={{0,2},{2,0},{4,6},{6,4},{1,3},{3,1},{5,7},{7,5},{8,10},{10,8},{12,... | collective-permute-start | bytes 1474568 | tf_op jit(solution)/shard_map/ppermute | solution.py:36
  267.0 22.6 %collective-permute-start.33 = (bf16[640,768]{1,0:T(8,128)(2,1)S(1)}, bf16[640,768]{1,0:T(8,128)(2,1)S(1)}, u32[]{:S(2)}, u32[]{:S(2)}) collective-permute-start(bf16[640,768]{1,0:T(8,128)(2,1)S(1)} %pad_maximum_fusion.refs_0_), channel_id=1, source_target_pairs={{0,16},{8,24},{16,0},{24,8},{1,17},{9,25},{17,1},{25,9},{2,18},{10... | collective-permute-start | bytes 2949128 | tf_op jit(solution)/shard_map/ppermute | solution.py:36
  268.3 22.4 %collective-permute-start.32 = (bf16[640,768]{1,0:T(8,128)(2,1)S(1)}, bf16[640,768]{1,0:T(8,128)(2,1)}, u32[]{:S(2)}, u32[]{:S(2)}) collective-permute-start(bf16[640,768]{1,0:T(8,128)(2,1)S(1)} %pad_maximum_fusion.refs_0_), channel_id=1, source_target_pairs={{0,8},{8,0},{16,24},{24,16},{1,9},{9,1},{17,25},{25,17},{2,10},{10... | collective-permute-start | bytes 2949128 | tf_op jit(solution)/shard_map/ppermute | solution.py:36
  268.9 18.7 %collective-permute-start.34 = (bf16[256,768]{1,0:T(8,128)(2,1)S(1)}, bf16[256,768]{1,0:T(8,128)(2,1)S(1)}, u32[]{:S(2)}, u32[]{:S(2)}) collective-permute-start(bf16[256,768]{1,0:T(8,128)(2,1)S(1)} %copy-done.7), channel_id=1, source_target_pairs={{0,4},{2,6},{4,0},{6,2},{1,5},{3,7},{5,1},{7,3},{8,12},{10,14},{12... | collective-permute-start | bytes 1179656 | tf_op jit(solution)/shard_map/ppermute | solution.py:36
  323.8 20.3 %collective-permute-start.43 = (bf16[384,768]{1,0:T(8,128)(2,1)S(1)}, bf16[384,768]{1,0:T(8,128)(2,1)S(1)}, u32[]{:S(2)}, u32[]{:S(2)}) collective-permute-start(bf16[384,768]{1,0:T(8,128)(2,1)S(1)} %pad_maximum_fusion.2.refs_0_), channel_id=1, source_target_pairs={{0,1},{1,0},{2,3},{3,2},{4,5},{5,4},{6,7},{7,6},{8,9},{9,8},{10,11... | collective-permute-start | bytes 1769480 | tf_op jit(solution)/shard_map/ppermute | solution.py:36
  323.8 20.3 %collective-permute-start.45 = (bf16[384,768]{1,0:T(8,128)(2,1)S(1)}, bf16[384,768]{1,0:T(8,128)(2,1)S(1)}, u32[]{:S(2)}, u32[]{:S(2)}) collective-permute-start(bf16[384,768]{1,0:T(8,128)(2,1)S(1)} %collective-permute-done.39.refs_2_), channel_id=1, source_target_pairs={{0,1},{1,0},{2,3},{3,2},{4,5},{5,4},{6,7},{7,6},{8,9},{9,8},{10,11... | collective-permute-start | bytes 1769480 | tf_op jit(solution)/shard_map/ppermute | solution.py:36
  (69 other events, 585.7 us)
where the time goes:
time: 356 us; the launch traced here: 352 us
  Pallas kernels  188 us (53%)
  waiting for transfers between devices  91.8 us (26%)
  starting transfers between devices  46.8 us (13%)
  local copies, waits for them, and re-layouts  12.9 us (4%)
  other arithmetic  8.32 us (2%)
    ppermute x48, waiting for transfers between devices, swapped(): return lax.ppermute(block, axis, [(i, i ^ distance) for i in range(count)])  91.8 us
    ppermute x48, starting transfers between devices, swapped(): return lax.ppermute(block, axis, [(i, i ^ distance) for i in range(count)])  46.8 us
    pallas_call x2, Pallas kernels, attention_backward(): pl.pallas_call(functools.partial(backward_kernel, count, last), grid_spec...  45 us
    pallas_call x1, Pallas kernels, middle(): pl.pallas_call(functools.partial(middle_kernel, pages, count, span, chunk...  43.1 us
    pallas_call x2, Pallas kernels, attention_forward(): pl.pallas_call(functools.partial(forward_kernel, page, count), grid_spec=...  42.4 us
    pallas_call x4, Pallas kernels, local(): pl.pallas_call(kernel, in_specs=[pl.BlockSpec(memory_space=pltpu.SMEM)] +...  12.7 us
    pallas_call x2, Pallas kernels, finished(): pl.pallas_call(kernel, grid=(1,), in_specs=[pl.BlockSpec(memory_space=plt...  10.7 us
    unnamed x90, local copies, waits for them, and re-layouts  8.75 us
  transfers between devices with their start and end apart: 48, of which 20 were waited for; matrix products, arithmetic and copies ran while one was open for 3% of the time, Pallas kernels for 38%

commit v1 on v0

--- a/solution.py
+++ b/solution.py
@@ -871,11 +871,8 @@
         )
 
     def sum_b(self, words, part_b, messages):
-        def body(words, ins, outs):
-            terms = [ref[: self.b].astype(F32) for ref in ins]
-            outs[0][...] = tree_sum(terms).astype(BF16)
-
-        return local(body, "sum_b", words, [part_b, *messages], self.shapes(self.b))[0]
+        terms = [after(words, part_b)] + [item[: self.b] for item in messages]
+        return tree_sum([item.astype(F32) for item in terms]).astype(BF16)
 
     def gather_b(self, words, part_b):
         for level in range(self.levels - 1, 0, -1):

time: 356 us -> 354 us (level)
    pallas_call x4 -> x3, Pallas kernels: 12.7 us -> 9.82 us  [local(): pl.pallas_call(kernel, in_specs=[pl.BlockSpec(memory_space=pltpu.SMEM)] +...]
    unnamed x90 -> x88, local copies, waits for them, and re-layouts: 8.75 us -> 7.45 us
  transfers between devices with their start and end apart: 48 -> 48, of which waited for: 20 -> 19; matrix products, arithmetic and copies ran while one was open for 3% -> 4% of each run, Pallas kernels for 38% -> 38%
where the time goes in v1:
time: 354 us; the launch traced here: 349 us
  Pallas kernels  186 us (53%)
  waiting for transfers between devices  91.7 us (26%)
  starting transfers between devices  46.4 us (13%)
  local copies, waits for them, and re-layouts  11.6 us (3%)
  other arithmetic  10.5 us (3%)
    ppermute x48, waiting for transfers between devices, swapped(): return lax.ppermute(block, axis, [(i, i ^ distance) for i in range(count)])  91.7 us
    ppermute x48, starting transfers between devices, swapped(): return lax.ppermute(block, axis, [(i, i ^ distance) for i in range(count)])  46.4 us
    pallas_call x2, Pallas kernels, attention_backward(): pl.pallas_call(functools.partial(backward_kernel, count, last), grid_spec...  45 us
    pallas_call x1, Pallas kernels, middle(): pl.pallas_call(functools.partial(middle_kernel, pages, count, span, chunk...  43.1 us
    pallas_call x2, Pallas kernels, attention_forward(): pl.pallas_call(functools.partial(forward_kernel, page, count), grid_spec=...  42.3 us
    pallas_call x2, Pallas kernels, finished(): pl.pallas_call(kernel, grid=(1,), in_specs=[pl.BlockSpec(memory_space=plt...  10.7 us
    pallas_call x3, Pallas kernels, local(): pl.pallas_call(kernel, in_specs=[pl.BlockSpec(memory_space=pltpu.SMEM)] +...  9.82 us
    pallas_call x1, Pallas kernels, widen_own(): pl.pallas_call(kernel, in_specs=[pl.BlockSpec(memory_space=pltpu.SMEM)] +...  8.66 us
  transfers between devices with their start and end apart: 48, of which 19 were waited for; matrix products, arithmetic and copies ran while one was open for 4% of the time, Pallas kernels for 38%

profile of v1, /device:TPU:0, one launch (start us, length us, event | category | flops | bytes accessed | tf_op | source)
XLA Modules:
  0.0 349.2 jit_solution(10240771374389094511)
XLA Ops:
  2.7 4.0 %collective-permute-start.2 = (bf16[272,768]{1,0:T(8,128)(2,1)S(1)}, bf16[272,768]{1,0:T(8,128)(2,1)S(1)}, u32[]{:S(2)}, u32[]{:S(2)}) collective-permute-start(bf16[272,768]{1,0:T(8,128)(2,1)S(1)} %fusion.1.refs_0_.refs_4_), channel_id=1, source_target_pairs={{0,24},{8,16},{16,8},{24,0},{1,25},{9,17},{17,9},{25,1},{2,26},{10... | collective-permute-start | bytes 1253384 | tf_op jit(solution)/shard_map/ppermute | solution.py:36
  8.0 4.9 %prepare.1 = (bf16[576,768]{1,0:T(8,128)(2,1)}, bf16[192,768]{1,0:T(8,128)(2,1)}, f32[32,1024]{1,0:T(8,128)}, f32[32,1024]{1,0:T(8,128)}) custom-call(s32[3]{0:T(128)} %pad_add_fusion.1.words_ref.refs_0_, bf16[768,768]{1,0:T(8,128)(2,1)} %refs_6_.1, bf16[768,768]{1,0:T(8,128)(2,1)} %refs_7_.1, bf16[768,768]{1,0:T(8,128)(2,1)} %refs_8_.3, ...), custom_call_target="tpu_custom_call" | custom-call | flops 905969664 | bytes 5898240 | tf_op jit(solution)/shard_map/prepare/pallas_call | solution.py:121
  12.9 4.3 %collective-permute-done.2.refs_3_.refs_7_ = bf16[272,768]{1,0:T(8,128)(2,1)S(1)} collective-permute-done((bf16[272,768]{1,0:T(8,128)(2,1)S(1)}, bf16[272,768]{1,0:T(8,128)(2,1)S(1)}, u32[]{:S(2)}, u32[]{:S(2)}) %collective-permute-start.2) | collective-permute-done | bytes 417824 | tf_op jit(solution)/shard_map/ppermute | solution.py:36
  17.2 8.1 %collective-permute-done.1.refs_2_.refs_6_ = bf16[272,768]{1,0:T(8,128)(2,1)S(1)} collective-permute-done((bf16[272,768]{1,0:T(8,128)(2,1)S(1)}, bf16[272,768]{1,0:T(8,128)(2,1)S(1)}, u32[]{:S(2)}, u32[]{:S(2)}) %collective-permute-start.1) | collective-permute-done | bytes 417824 | tf_op jit(solution)/shard_map/ppermute | solution.py:36
  29.1 21.2 %attention_forward.2 = (bf16[3,1024,1024]{2,1,0:T(8,128)(2,1)}, f32[3,64,1024]{2,1,0:T(8,128)}, bf16[3,256,1024]{2,1,0:T(8,128)(2,1)}, f32[384,1024]{1,0:T(8,128...) custom-call(s32[3]{0:T(128)} %pad_add_fusion.1.words_ref.refs_0_, ...), custom_call_target="tpu_custom_call" | custom-call | flops 8166309888 | bytes 15728640 | tf_op jit(solution)/shard_map/attention_forward/pallas_call | solution.py:261
  55.3 21.2 %attention_forward.3 = (bf16[3,1024,1024]{2,1,0:T(8,128)(2,1)}, f32[3,64,1024]{2,1,0:T(8,128)}, bf16[3,256,1024]{2,1,0:T(8,128)(2,1)}, f32[384,1024]{1,0:T(8,128...) custom-call(s32[3]{0:T(128)} %pad_add_fusion.1.words_ref.refs_0_, ...), custom_call_target="tpu_custom_call" | custom-call | flops 8166309888 | bytes 15728640 | tf_op jit(solution)/shard_map/attention_forward/pallas_call | solution.py:261
  85.1 43.1 %middle.1 = (bf16[512,768]{1,0:T(8,128)(2,1)}, f32[512,768]{1,0:T(8,128)}, bf16[3072,768]{1,0:T(8,128)(2,1)}, bf16[3072,768]{1,0:T(8,128)(2,1)}, bf16[512,768]{1...) custom-call(s32[3]{0:T(128)} %pad_add_fusion.1.words_ref.refs_0_, ...), custom_call_target="tpu_custom_call" | custom-call | flops 16307453952 | bytes 25165824 | tf_op jit(solution)/shard_map/middle/pallas_call | solution.py:623
  132.3 4.5 %collective-permute-done.12.refs_1_ = bf16[192,512]{1,0:T(8,128)(2,1)S(1)} collective-permute-done((bf16[192,512]{1,0:T(8,128)(2,1)}, bf16[192,512]{1,0:T(8,128)(2,1)S(1)}, u32[]{:S(2)}, u32[]{:S(2)}) %collective-permute-start.12) | collective-permute-done | bytes 196640 | tf_op jit(solution)/shard_map/ppermute | solution.py:36
  137.7 7.9 %scatter_one.1 = (bf16[640,768]{1,0:T(8,128)(2,1)}, bf16[640,768]{1,0:T(8,128)(2,1)}, bf16[640,768]{1,0:T(8,128)(2,1)}, bf16[640,768]{1,0:T(8,128)(2,1)}, bf16[5...) custom-call(s32[3]{0:T(128)} %pad_add_fusion.1.words_ref.refs_0_, bf16[3072,768]{1,0:T(8,128)(2,1)} %get-tuple-element.145.refs_0_.refs_4_, ...), custom_call_target="tpu_custom_call" | custom-call | tf_op jit(solution)/shard_map/scatter_one/pallas_call | solution.py:824
  150.8 22.0 %attention_backward.2 = (bf16[192,768]{1,0:T(8,128)(2,1)}, bf16[192,768]{1,0:T(8,128)(2,1)}, bf16[192,768]{1,0:T(8,128)(2,1)}, bf16[192,768]{1,0:T(8,128)(2,1)}, f32[768,768]{1,0:T(8,128)}) custom-call(s32[3]{0:T(128)} %pad_add_fusion.1.words_ref.refs_0_, bf16[192,512]{1,0:T(8,128)(2,1)} %get-tuple-element.142.refs_0_, bf16[192,512]{1,0:T(8,128)(2,1)} %copy-done.36, ...), custom_call_target="tpu_custom_call" | custom-call | flops 10355736576 | bytes 15728640 | tf_op jit(solution)/shard_map/attention_backward/pallas_call | solution.py:409
  178.7 23.0 %attention_backward.3 = (bf16[192,768]{1,0:T(8,128)(2,1)}, bf16[192,768]{1,0:T(8,128)(2,1)}, bf16[192,768]{1,0:T(8,128)(2,1)}, bf16[192,768]{1,0:T(8,128)(2,1)},...) custom-call(s32[3]{0:T(128)} %pad_add_fusion.1.words_ref.refs_0_, bf16[192,512]{1,0:T(8,128)(2,1)} %get-tuple-element.142.refs_0_, ...), custom_call_target="tpu_custom_call" | custom-call | flops 10355736576 | bytes 15728640 | tf_op jit(solution)/shard_map/attention_backward/pallas_call | solution.py:409
  203.4 5.2 %scatter_two.1 = (bf16[320,768]{1,0:T(8,128)(2,1)}, bf16[320,768]{1,0:T(8,128)(2,1)}, bf16[256,768]{1,0:T(8,128)(2,1)}, bf16[640,768]{1,0:T(8,128)(2,1)}, bf16[6...) custom-call(s32[3]{0:T(128)} %pad_add_fusion.1.words_ref.refs_0_, bf16[640,768]{1,0:T(8,128)(2,1)} %get-tuple-element.149.refs_0_, ...), custom_call_target="tpu_custom_call" | custom-call | tf_op jit(solution)/shard_map/scatter_two/pallas_call | solution.py:718
  212.5 8.1 %collective-permute-done.23 = bf16[320,768]{1,0:T(8,128)(2,1)S(1)} collective-permute-done((bf16[320,768]{1,0:T(8,128)(2,1)}, bf16[320,768]{1,0:T(8,128)(2,1)S(1)}, u32[]{:S(2)}, u32[]{:S(2)}) %collective-permute-start.23) | collective-permute-done | bytes 491552 | tf_op jit(solution)/shard_map/ppermute | solution.py:36
  225.0 19.3 %collective-permute-done.26 = bf16[320,768]{1,0:T(8,128)(2,1)} collective-permute-done((bf16[320,768]{1,0:T(8,128)(2,1)S(1)}, bf16[320,768]{1,0:T(8,128)(2,1)}, u32[]{:S(2)}, u32[]{:S(2)}) %collective-permute-start.26) | collective-permute-done | bytes 491552 | tf_op jit(solution)/shard_map/ppermute | solution.py:36
  247.5 5.9 %collective-permute-done.29.refs_4_ = bf16[640,768]{1,0:T(8,128)(2,1)S(1)} collective-permute-done((bf16[640,768]{1,0:T(8,128)(2,1)}, bf16[640,768]{1,0:T(8,128)(2,1)S(1)}, u32[]{:S(2)}, u32[]{:S(2)}) %collective-permute-start.29) | collective-permute-done | bytes 983072 | tf_op jit(solution)/shard_map/ppermute | solution.py:36
  254.9 7.9 %collective-permute-done.25 = bf16[192,768]{1,0:T(8,128)(2,1)S(1)} collective-permute-done((bf16[192,768]{1,0:T(8,128)(2,1)S(1)}, bf16[192,768]{1,0:T(8,128)(2,1)S(1)}, u32[]{:S(2)}, u32[]{:S(2)}) %collective-permute-start.25) | collective-permute-done | bytes 294944 | tf_op jit(solution)/shard_map/ppermute | solution.py:36
  270.2 6.9 %input_gradient.1 = bf16[512,768]{1,0:T(8,128)(2,1)} custom-call(s32[3]{0:T(128)} %pad_add_fusion.1.words_ref.refs_0_, bf16[192,768]{1,0:T(8,128)(2,1)} %get-tuple-element.195.refs_1_, bf16[192,768]{1,0:T(8,128)(2,1)} %get-tuple-element.196.refs_2_, bf16[640,768]{1,0:T(8,128)(2,1)} %copy-done.4, bf16[640,768]{1,0:T(8,128)(2,1)} %copy-done.5, ...), custom_call_target="tpu_custom_call" | custom-call | flops 1811939328 | bytes 7471104 | tf_op jit(solution)/shard_map/input_gradient/pallas_call | solution.py:694
  280.8 6.4 %collective-permute-done.34 = bf16[256,768]{1,0:T(8,128)(2,1)S(1)} collective-permute-done((bf16[256,768]{1,0:T(8,128)(2,1)S(1)}, bf16[256,768]{1,0:T(8,128)(2,1)S(1)}, u32[]{:S(2)}, u32[]{:S(2)}) %collective-permute-start.34) | collective-permute-done | bytes 393248 | tf_op jit(solution)/shard_map/ppermute | solution.py:36
  293.5 11.0 %collective-permute-done.37.refs_6_ = bf16[512,768]{1,0:T(8,128)(2,1)S(1)} collective-permute-done((bf16[512,768]{1,0:T(8,128)(2,1)S(1)}, bf16[512,768]{1,0:T(8,128)(2,1)S(1)}, u32[]{:S(2)}, u32[]{:S(2)}) %collective-permute-start.37) | collective-permute-done | bytes 786464 | tf_op jit(solution)/shard_map/ppermute | solution.py:36
  307.8 8.7 %widen_own.1 = (bf16[3584,768]{1,0:T(8,128)(2,1)}, f32[768,3072]{1,0:T(8,128)}, f32[3072,768]{1,0:T(8,128)}) custom-call(s32[3]{0:T(128)} %pad_add_fusion.1.words_ref.refs_0_, bf16[640,768]{1,0:T(8,128)(2,1)} %copy-done, bf16[640,768]{1,0:T(8,128)(2,1)} %collective-permute-done.32.refs_1_, bf16[640,768]{1,0:T(8,128)(2,1)} %copy-done.2, ...), custom_call_target="tpu_custom_call" | custom-call | bytes 14155776 | tf_op jit(solution)/shard_map/widen_own/pallas_call | solution.py:966
  321.9 6.7 %collective-permute-done.40.refs_3_ = bf16[192,768]{1,0:T(8,128)(2,1)S(1)} collective-permute-done((bf16[192,768]{1,0:T(8,128)(2,1)S(1)}, bf16[192,768]{1,0:T(8,128)(2,1)S(1)}, u32[]{:S(2)}, u32[]{:S(2)}) %collective-permute-start.40) | collective-permute-done | bytes 294944 | tf_op jit(solution)/shard_map/ppermute | solution.py:36
  330.1 5.3 %finish.2 = (f32[768,768]{1,0:T(8,128)}, f32[768,768]{1,0:T(8,128)}, f32[768,768]{1,0:T(8,128)}, f32[768,768]{1,0:T(8,128)}, f32[768,768]{1,0:T(8,128)}) custom-call(s32[3]{0:T(128)} %pad_add_fusion.1.words_ref.refs_0_, bf16[384,768]{1,0:T(8,128)(2,1)} %copy-done.3, bf16[384,768]{1,0:T(8,128)(2,1)} %copy-done.8, bf16[384,768]{1,0:T(8,128)(2,1)} %copy-done.7, ...), custom_call_target="tpu_custom_call" | custom-call | bytes 9437184 | tf_op jit(solution)/shard_map/finish/pallas_call | solution.py:1079
  335.4 6.2 %widen_other.1 = (f32[768,3072]{1,0:T(8,128)}, f32[3072,768]{1,0:T(8,128)}) custom-call(s32[3]{0:T(128)} %pad_add_fusion.1.words_ref.refs_0_, bf16[3584,768]{1,0:T(8,128)(2,1)} %collective-permute-done.42.half_ref.refs_5_, f32[768,3072]{1,0:T(8,128)} %get-tuple-element.223.before_ref, ...), custom_call_target="tpu_custom_call", output_to_operand_aliasing={{0}: (2, {}), {1}: (3, {})} | custom-call | bytes 14155776 | tf_op jit(solution)/shard_map/widen_other/pallas_call | solution.py:1000
  343.6 5.4 %finish.3 = (f32[768,768]{1,0:T(8,128)}, f32[768,768]{1,0:T(8,128)}, f32[768,768]{1,0:T(8,128)}, f32[768,768]{1,0:T(8,128)}, f32[768,768]{1,0:T(8,128)}) custom-call(s32[3]{0:T(128)} %pad_add_fusion.1.words_ref.refs_0_, bf16[384,768]{1,0:T(8,128)(2,1)} %copy-done.15, ...), custom_call_target="tpu_custom_call", output_to_operand_aliasing={{0}: (7, {}), {1}: (8, {}), {2}: (9, {}), {3}: (10, {}), {4... | custom-call | bytes 9437184 | tf_op jit(solution)/shard_map/finish/pallas_call | solution.py:1079
  (207 shorter events, 78.8 us)
Async XLA Ops:
  25.6 26.9 %collective-permute-start.8 = (bf16[256,768]{1,0:T(8,128)(2,1)S(1)}, bf16[256,768]{1,0:T(8,128)(2,1)S(1)}, u32[]{:S(2)}, u32[]{:S(2)}) collective-permute-start(bf16[256,768]{1,0:T(8,128)(2,1)S(1)} %get-tuple-element.136.refs_4_), channel_id=1, source_target_pairs={{0,24},{8,16},{16,8},{24,0},{1,25},{9,17},{17,9},{25,1},{2,26},{10... | collective-permute-start | bytes 1179656 | tf_op jit(solution)/shard_map/ppermute | solution.py:36
  27.2 26.7 %collective-permute-start.7 = (bf16[256,768]{1,0:T(8,128)(2,1)S(1)}, bf16[256,768]{1,0:T(8,128)(2,1)S(1)}, u32[]{:S(2)}, u32[]{:S(2)}) collective-permute-start(bf16[256,768]{1,0:T(8,128)(2,1)S(1)} %get-tuple-element.136.refs_4_), channel_id=1, source_target_pairs={{0,16},{8,24},{16,0},{24,8},{1,17},{9,25},{17,1},{25,9},{2,18},{10... | collective-permute-start | bytes 1179656 | tf_op jit(solution)/shard_map/ppermute | solution.py:36
  28.5 25.3 %collective-permute-start.6 = (bf16[256,768]{1,0:T(8,128)(2,1)S(1)}, bf16[256,768]{1,0:T(8,128)(2,1)S(1)}, u32[]{:S(2)}, u32[]{:S(2)}) collective-permute-start(bf16[256,768]{1,0:T(8,128)(2,1)S(1)} %get-tuple-element.136.refs_4_), channel_id=1, source_target_pairs={{0,8},{8,0},{16,24},{24,16},{1,9},{9,1},{17,25},{25,17},{2,10},{10... | collective-permute-start | bytes 1179656 | tf_op jit(solution)/shard_map/ppermute | solution.py:36
  50.3 28.4 %collective-permute-start.3 = (bf16[192,256]{1,0:T(8,128)(2,1)}, bf16[192,256]{1,0:T(8,128)(2,1)S(1)}, u32[]{:S(2)}, u32[]{:S(2)}) collective-permute-start(bf16[192,256]{1,0:T(8,128)(2,1)} %get-tuple-element.133), channel_id=1, source_target_pairs={{0,8},{8,0},{16,24},{24,16},{1,9},{9,1},{17,25},{25,17},{2,10},{10... | collective-permute-start | bytes 294920 | tf_op jit(solution)/shard_map/ppermute | solution.py:36
  51.8 28.8 %collective-permute-start.4 = (bf16[192,256]{1,0:T(8,128)(2,1)}, bf16[192,256]{1,0:T(8,128)(2,1)S(1)}, u32[]{:S(2)}, u32[]{:S(2)}) collective-permute-start(bf16[192,256]{1,0:T(8,128)(2,1)} %get-tuple-element.134), channel_id=1, source_target_pairs={{0,16},{8,24},{16,0},{24,8},{1,17},{9,25},{17,1},{25,9},{2,18},{10... | collective-permute-start | bytes 294920 | tf_op jit(solution)/shard_map/ppermute | solution.py:36
  52.5 28.2 %collective-permute-start.5 = (bf16[192,256]{1,0:T(8,128)(2,1)}, bf16[192,256]{1,0:T(8,128)(2,1)S(1)}, u32[]{:S(2)}, u32[]{:S(2)}) collective-permute-start(bf16[192,256]{1,0:T(8,128)(2,1)} %get-tuple-element.135), channel_id=1, source_target_pairs={{0,24},{8,16},{16,8},{24,0},{1,25},{9,17},{17,9},{25,1},{2,26},{10... | collective-permute-start | bytes 294920 | tf_op jit(solution)/shard_map/ppermute | solution.py:36
  130.1 19.0 %collective-permute-start.15 = (bf16[192,512]{1,0:T(8,128)(2,1)}, bf16[192,512]{1,0:T(8,128)(2,1)S(1)}, u32[]{:S(2)}, u32[]{:S(2)}) collective-permute-start(bf16[192,512]{1,0:T(8,128)(2,1)} %get-tuple-element.151), channel_id=1, source_target_pairs={{0,16},{8,24},{16,0},{24,8},{1,17},{9,25},{17,1},{25,9},{2,18},{10... | collective-permute-start | bytes 589832 | tf_op jit(solution)/shard_map/ppermute | solution.py:36
  130.6 20.2 %collective-permute-start.16 = (bf16[192,512]{1,0:T(8,128)(2,1)}, bf16[192,512]{1,0:T(8,128)(2,1)}, u32[]{:S(2)}, u32[]{:S(2)}) collective-permute-start(bf16[192,512]{1,0:T(8,128)(2,1)} %get-tuple-element.152), channel_id=1, source_target_pairs={{0,24},{8,16},{16,8},{24,0},{1,25},{9,17},{17,9},{25,1},{2,26},{10... | collective-permute-start | bytes 589832 | tf_op jit(solution)/shard_map/ppermute | solution.py:36
  145.6 27.3 %collective-permute-start.17 = (bf16[512,768]{1,0:T(8,128)(2,1)}, bf16[512,768]{1,0:T(8,128)(2,1)S(1)}, u32[]{:S(2)}, u32[]{:S(2)}) collective-permute-start(bf16[512,768]{1,0:T(8,128)(2,1)} %get-tuple-element.162), channel_id=1, source_target_pairs={{0,2},{2,0},{4,6},{6,4},{1,3},{3,1},{5,7},{7,5},{8,10},{10,8},{12,... | collective-permute-start | bytes 2359304 | tf_op jit(solution)/shard_map/ppermute | solution.py:36
  147.3 54.3 %collective-permute-start.18 = (bf16[640,768]{1,0:T(8,128)(2,1)}, bf16[640,768]{1,0:T(8,128)(2,1)S(1)}, u32[]{:S(2)}, u32[]{:S(2)}) collective-permute-start(bf16[640,768]{1,0:T(8,128)(2,1)} %get-tuple-element.173), channel_id=1, source_target_pairs={{0,8},{8,0},{16,24},{24,16},{1,9},{9,1},{17,25},{25,17},{2,10},{10... | collective-permute-start | bytes 2949128 | tf_op jit(solution)/shard_map/ppermute | solution.py:36
  148.6 53.1 %collective-permute-start.19 = (bf16[640,768]{1,0:T(8,128)(2,1)}, bf16[640,768]{1,0:T(8,128)(2,1)S(1)}, u32[]{:S(2)}, u32[]{:S(2)}) collective-permute-start(bf16[640,768]{1,0:T(8,128)(2,1)} %get-tuple-element.174), channel_id=1, source_target_pairs={{0,16},{8,24},{16,0},{24,8},{1,17},{9,25},{17,1},{25,9},{2,18},{10... | collective-permute-start | bytes 2949128 | tf_op jit(solution)/shard_map/ppermute | solution.py:36
  149.1 52.6 %collective-permute-start.20 = (bf16[640,768]{1,0:T(8,128)(2,1)}, bf16[640,768]{1,0:T(8,128)(2,1)S(1)}, u32[]{:S(2)}, u32[]{:S(2)}) collective-permute-start(bf16[640,768]{1,0:T(8,128)(2,1)} %get-tuple-element.175), channel_id=1, source_target_pairs={{0,24},{8,16},{16,8},{24,0},{1,25},{9,17},{17,9},{25,1},{2,26},{10... | collective-permute-start | bytes 2949128 | tf_op jit(solution)/shard_map/ppermute | solution.py:36
  176.1 25.6 %collective-permute-start.21 = (bf16[256,768]{1,0:T(8,128)(2,1)}, bf16[256,768]{1,0:T(8,128)(2,1)S(1)}, u32[]{:S(2)}, u32[]{:S(2)}) collective-permute-start(bf16[256,768]{1,0:T(8,128)(2,1)} %get-tuple-element.176), channel_id=1, source_target_pairs={{0,4},{2,6},{4,0},{6,2},{1,5},{3,7},{5,1},{7,3},{8,12},{10,14},{12... | collective-permute-start | bytes 1179656 | tf_op jit(solution)/shard_map/ppermute | solution.py:36
  209.0 38.5 %collective-permute-start.28 = (bf16[640,768]{1,0:T(8,128)(2,1)}, bf16[640,768]{1,0:T(8,128)(2,1)S(1)}, u32[]{:S(2)}, u32[]{:S(2)}) collective-permute-start(bf16[640,768]{1,0:T(8,128)(2,1)} %get-tuple-element.197), channel_id=1, source_target_pairs={{0,8},{8,0},{16,24},{24,16},{1,9},{9,1},{17,25},{25,17},{2,10},{10... | collective-permute-start | bytes 2949128 | tf_op jit(solution)/shard_map/ppermute | solution.py:36
  210.3 43.1 %collective-permute-start.29 = (bf16[640,768]{1,0:T(8,128)(2,1)}, bf16[640,768]{1,0:T(8,128)(2,1)S(1)}, u32[]{:S(2)}, u32[]{:S(2)}) collective-permute-start(bf16[640,768]{1,0:T(8,128)(2,1)} %get-tuple-element.198), channel_id=1, source_target_pairs={{0,16},{8,24},{16,0},{24,8},{1,17},{9,25},{17,1},{25,9},{2,18},{10... | collective-permute-start | bytes 2949128 | tf_op jit(solution)/shard_map/ppermute | solution.py:36
  210.8 42.6 %collective-permute-start.30 = (bf16[640,768]{1,0:T(8,128)(2,1)}, bf16[640,768]{1,0:T(8,128)(2,1)S(1)}, u32[]{:S(2)}, u32[]{:S(2)}) collective-permute-start(bf16[640,768]{1,0:T(8,128)(2,1)} %get-tuple-element.199), channel_id=1, source_target_pairs={{0,24},{8,16},{16,8},{24,0},{1,25},{9,17},{17,9},{25,1},{2,26},{10... | collective-permute-start | bytes 2949128 | tf_op jit(solution)/shard_map/ppermute | solution.py:36
  221.8 22.5 %collective-permute-start.26 = (bf16[320,768]{1,0:T(8,128)(2,1)S(1)}, bf16[320,768]{1,0:T(8,128)(2,1)}, u32[]{:S(2)}, u32[]{:S(2)}) collective-permute-start(bf16[320,768]{1,0:T(8,128)(2,1)S(1)} %add.65), channel_id=1, source_target_pairs={{0,4},{2,6},{4,0},{6,2},{1,5},{3,7},{5,1},{7,3},{8,12},{10,14},{12... | collective-permute-start | bytes 1474568 | tf_op jit(solution)/shard_map/ppermute | solution.py:36
  224.5 21.0 %collective-permute-start.24 = (bf16[192,768]{1,0:T(8,128)(2,1)}, bf16[192,768]{1,0:T(8,128)(2,1)S(1)}, u32[]{:S(2)}, u32[]{:S(2)}) collective-permute-start(bf16[192,768]{1,0:T(8,128)(2,1)} %get-tuple-element.190), channel_id=1, source_target_pairs={{0,2},{2,0},{4,6},{6,4},{1,3},{3,1},{5,7},{7,5},{8,10},{10,8},{12,... | collective-permute-start | bytes 884744 | tf_op jit(solution)/shard_map/ppermute | solution.py:36
  245.4 21.0 %collective-permute-start.27 = (bf16[320,768]{1,0:T(8,128)(2,1)S(1)}, bf16[320,768]{1,0:T(8,128)(2,1)S(1)}, u32[]{:S(2)}, u32[]{:S(2)}) collective-permute-start(bf16[320,768]{1,0:T(8,128)(2,1)S(1)} %add.68), channel_id=1, source_target_pairs={{0,2},{2,0},{4,6},{6,4},{1,3},{3,1},{5,7},{7,5},{8,10},{10,8},{12,... | collective-permute-start | bytes 1474568 | tf_op jit(solution)/shard_map/ppermute | solution.py:36
  266.6 22.6 %collective-permute-start.33 = (bf16[640,768]{1,0:T(8,128)(2,1)S(1)}, bf16[640,768]{1,0:T(8,128)(2,1)S(1)}, u32[]{:S(2)}, u32[]{:S(2)}) collective-permute-start(bf16[640,768]{1,0:T(8,128)(2,1)S(1)} %pad_maximum_fusion.refs_0_), channel_id=1, source_target_pairs={{0,16},{8,24},{16,0},{24,8},{1,17},{9,25},{17,1},{25,9},{2,18},{10... | collective-permute-start | bytes 2949128 | tf_op jit(solution)/shard_map/ppermute | solution.py:36
  268.0 22.4 %collective-permute-start.32 = (bf16[640,768]{1,0:T(8,128)(2,1)S(1)}, bf16[640,768]{1,0:T(8,128)(2,1)}, u32[]{:S(2)}, u32[]{:S(2)}) collective-permute-start(bf16[640,768]{1,0:T(8,128)(2,1)S(1)} %pad_maximum_fusion.refs_0_), channel_id=1, source_target_pairs={{0,8},{8,0},{16,24},{24,16},{1,9},{9,1},{17,25},{25,17},{2,10},{10... | collective-permute-start | bytes 2949128 | tf_op jit(solution)/shard_map/ppermute | solution.py:36
  268.4 18.7 %collective-permute-start.34 = (bf16[256,768]{1,0:T(8,128)(2,1)S(1)}, bf16[256,768]{1,0:T(8,128)(2,1)S(1)}, u32[]{:S(2)}, u32[]{:S(2)}) collective-permute-start(bf16[256,768]{1,0:T(8,128)(2,1)S(1)} %add_convert_fusion), channel_id=1, source_target_pairs={{0,4},{2,6},{4,0},{6,2},{1,5},{3,7},{5,1},{7,3},{8,12},{10,14},{12... | collective-permute-start | bytes 1179656 | tf_op jit(solution)/shard_map/ppermute | solution.py:36
  321.3 20.3 %collective-permute-start.43 = (bf16[384,768]{1,0:T(8,128)(2,1)S(1)}, bf16[384,768]{1,0:T(8,128)(2,1)S(1)}, u32[]{:S(2)}, u32[]{:S(2)}) collective-permute-start(bf16[384,768]{1,0:T(8,128)(2,1)S(1)} %pad_maximum_fusion.2.refs_0_), channel_id=1, source_target_pairs={{0,1},{1,0},{2,3},{3,2},{4,5},{5,4},{6,7},{7,6},{8,9},{9,8},{10,11... | collective-permute-start | bytes 1769480 | tf_op jit(solution)/shard_map/ppermute | solution.py:36
  321.3 20.3 %collective-permute-start.45 = (bf16[384,768]{1,0:T(8,128)(2,1)S(1)}, bf16[384,768]{1,0:T(8,128)(2,1)S(1)}, u32[]{:S(2)}, u32[]{:S(2)}) collective-permute-start(bf16[384,768]{1,0:T(8,128)(2,1)S(1)} %collective-permute-done.39.refs_2_), channel_id=1, source_target_pairs={{0,1},{1,0},{2,3},{3,2},{4,5},{5,4},{6,7},{7,6},{8,9},{9,8},{10,11... | collective-permute-start | bytes 1769480 | tf_op jit(solution)/shard_map/ppermute | solution.py:36
  (68 other events, 619.2 us)
